TPU v7x, 32 devices: a whole 2x2x4 slice. The times are simulated.
32 devices in a mesh: rep: 4 (over y, x), fsdp: 8 (over z, core).
Axes of the slice: x: 2, y: 2, z: 4, core: 2. Of those that a mesh axis runs over, the one named last changes fastest.
Arguments:
- tokens: bfloat16 [32768, 768], P(('rep', 'fsdp')), may hold values from -6 to 6
- exit_layer: int32 [256], P(('rep', 'fsdp')), may hold values from 1 to 12
- qkv_weight: bfloat16 [768, 2304], P('fsdp'), may hold values from -0.21875 to 0.21875
- query_bias: bfloat16 [768], P('fsdp'), may hold values from -3 to 3
- value_bias: bfloat16 [768], P('fsdp'), may hold values from -3 to 3
- out_weight: bfloat16 [768, 768], P('fsdp'), may hold values from -0.625 to 0.625
- out_bias: bfloat16 [768], P('fsdp'), may hold values from -3 to 3
- attn_gain: bfloat16 [768], P('fsdp'), may hold values from 0.099609375 to 1.8984375
- attn_shift: bfloat16 [768], P('fsdp'), may hold values from -3 to 3
- up_weight: bfloat16 [768, 3072], P('fsdp'), may hold values from -0.21875 to 0.21875
- up_bias: bfloat16 [3072], P('fsdp'), may hold values from -3 to 3
- down_weight: bfloat16 [3072, 768], P('fsdp'), may hold values from -0.109375 to 0.109375
- down_bias: bfloat16 [768], P('fsdp'), may hold values from -3 to 3
- block_gain: bfloat16 [768], P('fsdp'), may hold values from 0.099609375 to 1.8984375
- block_shift: bfloat16 [768], P('fsdp'), may hold values from -3 to 3
- pool_weight: bfloat16 [768, 768], P('fsdp'), may hold values from -0.21875 to 0.21875
- pool_bias: bfloat16 [768], P('fsdp'), may hold values from -3 to 3
- class_weight: bfloat16 [768, 3], P('fsdp'), may hold values from -0.875 to 0.875
- class_bias: bfloat16 [3], replicated, may hold values from -4 to 4
- output_grad: bfloat16 [32768, 768], P(('rep', 'fsdp')), may hold values from -6 to 6
- logit_grad: bfloat16 [256, 3], P(('rep', 'fsdp')), may hold values from -6 to 6
Outputs:
- output: bfloat16 [32768, 768], P(('rep', 'fsdp'))
- logits: float32 [256, 3], P(('rep', 'fsdp'))
- entropy_mean: float32 [], replicated
- input_grad: bfloat16 [32768, 768], P(('rep', 'fsdp'))
- qkv_weight_grad: float32 [768, 2304], P('fsdp')
- query_bias_grad: float32 [768], P('fsdp')
- value_bias_grad: float32 [768], P('fsdp')
- out_weight_grad: float32 [768, 768], P('fsdp')
- out_bias_grad: float32 [768], P('fsdp')
- attn_gain_grad: float32 [768], P('fsdp')
- attn_shift_grad: float32 [768], P('fsdp')
- up_weight_grad: float32 [768, 3072], P('fsdp')
- up_bias_grad: float32 [3072], P('fsdp')
- down_weight_grad: float32 [3072, 768], P('fsdp')
- down_bias_grad: float32 [768], P('fsdp')
- block_gain_grad: float32 [768], P('fsdp')
- block_shift_grad: float32 [768], P('fsdp')
- pool_weight_grad: float32 [768, 768], P('fsdp')
- pool_bias_grad: float32 [768], P('fsdp')
- class_weight_grad: float32 [768, 3], P('fsdp')
- class_bias_grad: float32 [3], replicated
Inputs may be any that keep to these rules, and one draw needn't show every extreme that they name: `exit_layer`: the last layer that each sequence passes; this layer is number 6.
All inputs are finite; a program needn't handle non-finite values.
Results may differ from a plain program's by a relative error of at most 0.02.
Values may be sent and summed in bfloat16 or wider, within the bound.
No kernel may reach another device: no remote copies, remote signals or barrier semaphores. Data moves between devices by JAX's collectives and lax.ppermute only.
A program may use at most 192 MiB of HBM per device.

v0:
```python
import functools
import math

import jax
import jax.numpy as jnp
from jax import lax
from jax.experimental import pallas as pl
from jax.experimental.pallas import tpu as pltpu
from jax.sharding import PartitionSpec as P

HD = 64
LAYER = 6
PAIR = 2 * HD
NEAR = (1, 2)
FAR = 3
LANES = 128
VMEM_BYTES = 58 * 2**20
BF = jnp.bfloat16
F32 = jnp.float32

QUERY_BIAS, VALUE_BIAS, OUT_BIAS, ATTN_GAIN, ATTN_SHIFT = 0, 1, 2, 3, 4
DOWN_BIAS, BLOCK_GAIN, BLOCK_SHIFT, CLASS_ROWS, POOL_BIAS = 5, 6, 7, 8, 11
VECTOR_ROWS = 12


def nn(left, right):
    return jnp.dot(left, right, preferred_element_type=F32)


def tn(left, right):
    return lax.dot_general(left, right, (((0,), (0,)), ((), ())), preferred_element_type=F32)


def nt(left, right):
    return lax.dot_general(left, right, (((1,), (1,)), ((), ())), preferred_element_type=F32)


def full(shape):
    return pl.BlockSpec(shape, lambda *at: (0,) * len(shape))


def params():
    return pltpu.CompilerParams(
        dimension_semantics=("arbitrary",), vmem_limit_bytes=VMEM_BYTES
    )


def cost(flops, moved, trans=0):
    return pl.CostEstimate(flops=flops, bytes_accessed=moved, transcendentals=trans)


def split_heads(pair):
    lane = lax.broadcasted_iota(jnp.int32, pair.shape, 1)
    zero = jnp.zeros_like(pair)
    return jnp.concatenate(
        [jnp.where(lane < HD, pair, zero), jnp.where(lane < HD, zero, pair)], axis=0
    )


def norm_stats(values):
    center = values - jnp.mean(values, axis=-1, keepdims=True)
    spread = jnp.mean(center * center, axis=-1, keepdims=True)
    scale = lax.rsqrt(spread + 1e-06)
    return center * scale, scale


def norm_back(grad, unit, scale, gain):
    inner = grad * gain
    first = jnp.mean(inner, axis=-1, keepdims=True)
    second = jnp.mean(inner * unit, axis=-1, keepdims=True)
    return scale * (inner - first - unit * second)


def gelu_parts(values):
    base = 1.0 + 0.23164189 * jnp.abs(values)
    t = pl.reciprocal(base, approx=True)
    t = t * (2.0 - base * t)
    bell = jnp.exp2((values * values) * -0.7213475204444817)
    poly = t * (
        0.127414796
        + t * (-0.142248368 + t * (0.7107068705 + t * (-0.7265760135 + t * 0.5307027145)))
    )
    tail = poly * bell
    below = jnp.where(values >= 0.0, 1.0 - tail, tail)
    return values * below, below + values * (bell * 0.3989422804014327)


def attend_kernel(length, tok_ref, w_ref, vec_ref, joined_ref, probs_ref, ctx_ref):
    rows, width = ctx_ref.shape
    pairs = width // PAIR
    for part in range(3):
        cols = slice(part * width, (part + 1) * width)
        value = nn(tok_ref[...], w_ref[part])
        if part == 0:
            value += vec_ref[QUERY_BIAS : QUERY_BIAS + 1]
        elif part == 2:
            value += vec_ref[VALUE_BIAS : VALUE_BIAS + 1]
        joined_ref[:, cols] = value.astype(BF)

    def one(seq, carry):
        at = pl.ds(pl.multiple_of(seq * length, length), length)
        scores = []
        for pair in range(pairs):
            query = joined_ref[at, pair * PAIR : (pair + 1) * PAIR] * jnp.asarray(0.125, BF)
            keys = split_heads(joined_ref[at, width + pair * PAIR : width + (pair + 1) * PAIR])
            scores.append(nt(keys, query))
        all_probs = []
        for pair in range(pairs):
            halves = []
            for head in range(2):
                part = scores[pair][head * length : (head + 1) * length]
                part = jnp.exp(part - jnp.max(part, axis=0, keepdims=True))
                part = part * (1.0 / jnp.sum(part, axis=0, keepdims=True))
                halves.append(part.astype(BF))
            probs = jnp.concatenate(halves, axis=0)
            probs_ref[seq, pair] = probs
            all_probs.append(probs)
        for pair in range(pairs):
            vals = split_heads(
                joined_ref[at, 2 * width + pair * PAIR : 2 * width + (pair + 1) * PAIR]
            )
            ctx_ref[at, pair * PAIR : (pair + 1) * PAIR] = tn(all_probs[pair], vals).astype(BF)
        return carry

    lax.fori_loop(0, rows // length, one, 0)


def attend(tokens, qkv, vec, length):
    rows, width = tokens.shape
    count = rows // length
    steps = 2
    block = rows // steps
    pairs = width // PAIR
    return pl.pallas_call(
        functools.partial(attend_kernel, length),
        grid=(steps,),
        in_specs=[
            pl.BlockSpec((block, width), lambda i: (i, 0)),
            full((3, width, width)),
            full(vec.shape),
        ],
        out_specs=[
            pl.BlockSpec((block, 3 * width), lambda i: (i, 0)),
            pl.BlockSpec((count // steps, pairs, 2 * length, length), lambda i: (i, 0, 0, 0)),
            pl.BlockSpec((block, width), lambda i: (i, 0)),
        ],
        out_shape=[
            jax.ShapeDtypeStruct((rows, 3 * width), BF),
            jax.ShapeDtypeStruct((count, pairs, 2 * length, length), BF),
            jax.ShapeDtypeStruct((rows, width), BF),
        ],
        compiler_params=params(),
        cost_estimate=cost(8 * rows * width * width, 20 * rows * width, rows * width),
        name="attend",
    )(tokens, qkv, vec)


def feed_kernel(
    length,
    load,
    inputs,
    place_ref,
    exit_ref,
    tok_ref,
    ctx_ref,
    out_w_ref,
    vec_ref,
    up_b_ref,
    *refs,
):
    weights, refs = refs[:inputs], refs[inputs:]
    (
        turned_ref,
        act_ref,
        slope_ref,
        unit1_ref,
        scale1_ref,
        unit2_ref,
        scale2_ref,
        output_ref,
        *more,
        acc_ref,
        low_ref,
        line_ref,
    ) = refs[: 11 + (2 if load else 0)]
    step = pl.program_id(0)
    last = pl.num_programs(0) - 1
    rows, width = tok_ref.shape
    sub = 256
    if load:
        up_all, down_all, sems, out_sems = refs[13:]
        each = down_all.shape[0] // up_all.shape[0]
        stores = [
            pltpu.make_async_copy(up_all, more[0], out_sems.at[0]),
            pltpu.make_async_copy(down_all, more[1], out_sems.at[1]),
        ]

        def up_part(cols):
            return up_all[step, :, cols]

        def down_part(cols):
            return down_all[pl.ds(step * each, each), :, cols].reshape(width, sub)

    else:

        def up_part(cols):
            return weights[0][0, :, cols]

        def down_part(cols):
            return weights[1][:, :, cols].reshape(width, sub)

    @pl.when(step == 0)
    def _():
        if load:
            copies = load(weights, up_all, down_all, place_ref, sems)
        for m in range(rows // sub):
            at = slice(m * sub, (m + 1) * sub)
            inner = tok_ref[at].astype(F32) + (
                nn(ctx_ref[at], out_w_ref[0]) + vec_ref[OUT_BIAS : OUT_BIAS + 1]
            )
            unit, scale = norm_stats(inner)
            first = unit * vec_ref[ATTN_GAIN : ATTN_GAIN + 1] + vec_ref[ATTN_SHIFT : ATTN_SHIFT + 1]
            unit1_ref[at] = unit.astype(BF)
            scale1_ref[at] = scale
            low = first.astype(BF)
            low_ref[at] = low
            turned_ref[:, at] = low.T
            acc_ref[at] = first + vec_ref[DOWN_BIAS : DOWN_BIAS + 1]
        if load:
            for copy in copies:
                copy.wait()
            for store in stores:
                store.start()

    tiles = [(m, n) for m in range(rows // sub) for n in range(width // sub)]

    def rows_of(m):
        return slice(m * sub, (m + 1) * sub)

    def first_product(tile):
        return nn(low_ref[rows_of(tile[0])], up_part(rows_of(tile[1])))

    def second_product(m, n):
        at, cols = rows_of(m), rows_of(n)
        acc_ref[at, cols] += nn(line_ref[m % 2], down_part(cols))

    ahead = first_product(tiles[0])
    for index, (m, n) in enumerate(tiles):
        at, cols = rows_of(m), rows_of(n)
        hidden = ahead + up_b_ref[:, cols]
        if index + 1 < len(tiles):
            ahead = first_product(tiles[index + 1])
        if m > 0:
            second_product(m - 1, n)
        act, slope = gelu_parts(hidden)
        act = act.astype(BF)
        line_ref[m % 2, :, cols] = act
        act_ref[cols, at] = act.T
        slope_ref[at, cols] = slope.astype(BF)
    for n in range(width // sub):
        second_product(rows // sub - 1, n)

    @pl.when(step == last)
    def _():
        for seq in range(rows // length):
            at = slice(seq * length, (seq + 1) * length)
            active = (exit_ref[seq] >= LAYER).astype(F32)
            unit, scale = norm_stats(acc_ref[at])
            unit2_ref[at] = unit.astype(BF)
            scale2_ref[at] = scale
            result = (
                unit * vec_ref[BLOCK_GAIN : BLOCK_GAIN + 1] + vec_ref[BLOCK_SHIFT : BLOCK_SHIFT + 1]
            ) * active
            output_ref[at] = result.astype(BF)
        if load:
            for store in stores:
                store.wait()


def feed(place, exit_layer, tokens, ctx, out_w, vec, up_bias, weights, load, shapes, length):
    rows, width = tokens.shape
    hidden = up_bias.shape[1]
    steps = hidden // width
    whole = full((rows, width))
    if load:
        weight_specs = [pl.BlockSpec(memory_space=pl.ANY)] * len(weights)
        more_specs = [pl.BlockSpec(memory_space=pl.ANY)] * 2
        more = [jax.ShapeDtypeStruct(shape, BF) for shape in shapes]
        copies = 2 * shapes[1][0] * shapes[0][0]
        scratch = [pltpu.VMEM(shape, BF) for shape in shapes] + [
            pltpu.SemaphoreType.DMA((copies,)),
            pltpu.SemaphoreType.DMA((2,)),
        ]
    else:
        weight_specs = [
            pl.BlockSpec((1, width, width), lambda i: (i, 0, 0)),
            pl.BlockSpec((1, width, width), lambda i: (i, 0, 0)),
        ]
        more_specs, more, scratch = [], [], []
    return pl.pallas_call(
        functools.partial(feed_kernel, length, load, len(weights)),
        grid=(steps,),
        in_specs=[
            pl.BlockSpec(memory_space=pltpu.SMEM),
            pl.BlockSpec(memory_space=pltpu.SMEM),
            whole,
            whole,
            pl.BlockSpec((1, width, width), lambda i: (3, 0, 0)),
            full(vec.shape),
            pl.BlockSpec((1, width), lambda i: (0, i)),
        ]
        + weight_specs,
        out_specs=[
            full((width, rows)),
            pl.BlockSpec((width, rows), lambda i: (i, 0)),
            pl.BlockSpec((rows, width), lambda i: (0, i)),
            whole,
            full((rows, 1)),
            whole,
            full((rows, 1)),
            whole,
        ]
        + more_specs,
        out_shape=[
            jax.ShapeDtypeStruct((width, rows), BF),
            jax.ShapeDtypeStruct((hidden, rows), BF),
            jax.ShapeDtypeStruct((rows, hidden), BF),
            jax.ShapeDtypeStruct((rows, width), BF),
            jax.ShapeDtypeStruct((rows, 1), F32),
            jax.ShapeDtypeStruct((rows, width), BF),
            jax.ShapeDtypeStruct((rows, 1), F32),
            jax.ShapeDtypeStruct((rows, width), BF),
        ]
        + more,
        scratch_shapes=[
            pltpu.VMEM((rows, width), F32),
            pltpu.VMEM((rows, width), BF),
            pltpu.VMEM((2, 256, width), BF),
        ]
        + scratch,
        compiler_params=params(),
        cost_estimate=cost(18 * rows * width * width, 40 * rows * width, 8 * rows * width),
        name="feed",
    )(place, exit_layer, tokens, ctx, out_w, vec, up_bias, *weights)


def load_second(counts, chips, reps, part, weights, up_all, down_all, place_ref, sems):
    at = 0
    groups = []
    for number in counts:
        groups.append(weights[at : at + number])
        at += number
    copies = []

    def start(source, target):
        copies.append(pltpu.make_async_copy(source, target, sems.at[len(copies)]))
        copies[-1].start()

    second_plan(
        start,
        groups,
        (up_all, down_all),
        place_ref[0],
        place_ref[1],
        place_ref[2],
        chips,
        reps,
        part,
    )
    return copies


def leave_kernel(
    length,
    classes,
    exit_ref,
    output_ref,
    unit2_ref,
    scale2_ref,
    grad_ref,
    pool_ref,
    vec_ref,
    class_bias_ref,
    logit_grad_ref,
    act_ref,
    outer_ref,
    branch_ref,
    joint_grad_ref,
    sums_ref,
    class_grad_ref,
    logits_ref,
    stats_ref,
    lead_ref,
    pool_grad_ref,
):
    step = pl.program_id(0)
    rows, width = output_ref.shape
    pool = pool_ref[...].reshape(width, width)
    count = rows // length

    @pl.when(step == 0)
    def _():
        place = lax.broadcasted_iota(jnp.int32, (count, 1), 0)
        active = jnp.zeros((count, 1), F32)
        for seq in range(count):
            on = (exit_ref[seq] >= LAYER).astype(F32)
            active = jnp.where(place == seq, on, active)
        leading = jnp.concatenate(
            [output_ref[seq * length : seq * length + 1].astype(F32) for seq in range(count)],
            axis=0,
        ).astype(BF)
        pooled = jnp.tanh(nn(leading, pool) + vec_ref[POOL_BIAS : POOL_BIAS + 1])
        pooled_low = pooled.astype(BF)
        used = lax.broadcasted_iota(jnp.int32, (8, width), 0) < classes
        class_rows = jnp.where(used, vec_ref[CLASS_ROWS : CLASS_ROWS + 8], 0.0).astype(BF)
        raw = nt(pooled_low, class_rows) + class_bias_ref[...]
        lane = lax.broadcasted_iota(jnp.int32, raw.shape, 1) < classes
        top = jnp.max(jnp.where(lane, raw, -jnp.inf), axis=-1, keepdims=True)
        spread = jnp.where(lane, jnp.exp(raw - top), 0.0)
        logprob = raw - top - jnp.log(jnp.sum(spread, axis=-1, keepdims=True))
        entropy = -jnp.sum(
            jnp.where(lane, jnp.exp(logprob) * logprob, 0.0), axis=-1, keepdims=True
        )
        logits_ref[...] = raw * active
        class_grad = (logit_grad_ref[...].astype(F32) * active).astype(BF)
        stats_ref[0:1] = jnp.broadcast_to(jnp.sum(entropy * active, axis=0, keepdims=True), (1, 8))
        stats_ref[1:2] = jnp.sum(class_grad.astype(F32), axis=0, keepdims=True)
        class_grad_ref[...] = tn(class_grad, pooled_low)
        pooled_grad = nn(class_grad, class_rows)
        pre_grad = (pooled_grad * (1.0 - pooled * pooled)).astype(BF)
        sums_ref[3:4] = jnp.sum(pre_grad.astype(F32), axis=0, keepdims=True)
        pool_grad_ref[...] = tn(leading, pre_grad).reshape(pool_grad_ref.shape).astype(BF)
        lead_ref[...] = nt(pre_grad, pool)
        head = lax.broadcasted_iota(jnp.int32, (length, 1), 0) == 0
        gain = vec_ref[BLOCK_GAIN : BLOCK_GAIN + 1]
        gain_sum = jnp.zeros((1, width), F32)
        shift_sum = jnp.zeros((1, width), F32)
        bias_sum = jnp.zeros((1, width), F32)
        for seq in range(count):
            at = slice(seq * length, (seq + 1) * length)
            on = (exit_ref[seq] >= LAYER).astype(F32)
            top_grad = (
                grad_ref[at].astype(F32) + jnp.where(head, lead_ref[seq : seq + 1], 0.0)
            ) * on
            unit = unit2_ref[at].astype(F32)
            outer = norm_back(top_grad, unit, scale2_ref[at], gain)
            branch = outer.astype(BF)
            outer_ref[at] = outer
            branch_ref[at] = branch
            gain_sum += jnp.sum(top_grad * unit, axis=0, keepdims=True)
            shift_sum += jnp.sum(top_grad, axis=0, keepdims=True)
            bias_sum += jnp.sum(branch.astype(F32), axis=0, keepdims=True)
        sums_ref[0:1] = gain_sum
        sums_ref[1:2] = shift_sum
        sums_ref[2:3] = bias_sum

    @pl.when(step > 0)
    def _():
        few, both, _ = joint_grad_ref.shape
        deep = width // few
        value = nn(act_ref[...], branch_ref[...])
        for at in range(few):
            joint_grad_ref[at, 0:deep] = value[at * deep : (at + 1) * deep].astype(BF)
            joint_grad_ref[at, deep:both] = pool_grad_ref[(step - 1) * few + at]


def leave(
    exit_layer, output, unit2, scale2, output_grad, pool, vec, class_bias, logit_grad, act,
    pool_spec, shards, length, classes,
):
    rows, width = output.shape
    count = rows // length
    hidden = act.shape[0]
    steps = hidden // width
    few = shards // steps
    both = (hidden + width) // shards
    whole = full((rows, width))
    return pl.pallas_call(
        functools.partial(leave_kernel, length, classes),
        grid=(steps + 1,),
        in_specs=[
            pl.BlockSpec(memory_space=pltpu.SMEM),
            whole,
            whole,
            full((rows, 1)),
            whole,
            pool_spec,
            full(vec.shape),
            full(class_bias.shape),
            full(logit_grad.shape),
            pl.BlockSpec((width, rows), lambda i: (jnp.maximum(i - 1, 0), 0)),
        ],
        out_specs=[
            whole,
            whole,
            pl.BlockSpec((few, both, width), lambda i: (jnp.maximum(i - 1, 0), 0, 0)),
            full((4, width)),
            full((8, width)),
            full((count, 8)),
            full((2, 8)),
        ],
        out_shape=[
            jax.ShapeDtypeStruct((rows, width), F32),
            jax.ShapeDtypeStruct((rows, width), BF),
            jax.ShapeDtypeStruct((shards, both, width), BF),
            jax.ShapeDtypeStruct((4, width), F32),
            jax.ShapeDtypeStruct((8, width), F32),
            jax.ShapeDtypeStruct((count, 8), F32),
            jax.ShapeDtypeStruct((2, 8), F32),
        ],
        scratch_shapes=[
            pltpu.VMEM((count, width), F32),
            pltpu.VMEM((shards, width // shards, width), BF),
        ],
        compiler_params=params(),
        cost_estimate=cost(8 * rows * width * width, 30 * rows * width),
        name="leave",
    )(
        exit_layer, output, unit2, scale2, output_grad, pool, vec, class_bias, logit_grad, act
    )


def split_cores(value, place_ref, keep_ref, send_ref):
    chips, part, _ = keep_ref.shape
    first = place_ref[2] == 0
    for chip in range(chips):
        even = value[2 * chip * part : (2 * chip + 1) * part]
        odd = value[(2 * chip + 1) * part : (2 * chip + 2) * part]
        keep_ref[chip] = jnp.where(first, even, odd).astype(BF)
        send_ref[chip] = jnp.where(first, odd, even).astype(BF)


def feed_back_kernel(
    place_ref,
    branch_ref,
    slope_ref,
    turned_ref,
    down_ref,
    up_ref,
    outer_ref,
    unit1_ref,
    scale1_ref,
    out_w_ref,
    vec_ref,
    ctx_ref,
    keep_ref,
    send_ref,
    up_sum_ref,
    inner_ref,
    attended_ref,
    ctx_grad_ref,
    sums_ref,
    acc_ref,
    hid_ref,
):
    step = pl.program_id(0)
    rows, width = branch_ref.shape
    sub = 512

    @pl.when(step == 0)
    def _():
        acc_ref[...] = outer_ref[...]

    last = pl.num_programs(0) - 1

    @pl.when(step < last)
    def _():
        total = jnp.zeros((1, width), F32)
        down = down_ref[...].reshape(up_ref.shape[1:])
        ahead = nt(branch_ref[0:sub], down)
        for m in range(rows // sub):
            at = slice(m * sub, (m + 1) * sub)
            hid = (ahead * slope_ref[at].astype(F32)).astype(BF)
            if (m + 1) * sub < rows:
                ahead = nt(branch_ref[(m + 1) * sub : (m + 2) * sub], down)
            hid_ref[at] = hid
            total += jnp.sum(hid.astype(F32), axis=0, keepdims=True)
            acc_ref[at] += nt(hid, up_ref[0])
        up_sum_ref[...] = total
        split_cores(nn(turned_ref[...], hid_ref[...]), place_ref, keep_ref, send_ref)

    @pl.when(step == last)
    def _():
        gain = vec_ref[ATTN_GAIN : ATTN_GAIN + 1]
        gain_sum = jnp.zeros((1, width), F32)
        shift_sum = jnp.zeros((1, width), F32)
        bias_sum = jnp.zeros((1, width), F32)
        for m in range(rows // sub):
            at = slice(m * sub, (m + 1) * sub)
            grad = acc_ref[at]
            unit = unit1_ref[at].astype(F32)
            inner = norm_back(grad, unit, scale1_ref[at], gain)
            attended = inner.astype(BF)
            inner_ref[at] = inner
            attended_ref[at] = attended
            ctx_grad_ref[at] = nt(attended, out_w_ref[0]).astype(BF)
            gain_sum += jnp.sum(grad * unit, axis=0, keepdims=True)
            shift_sum += jnp.sum(grad, axis=0, keepdims=True)
            bias_sum += jnp.sum(attended.astype(F32), axis=0, keepdims=True)
        sums_ref[0:1] = gain_sum
        sums_ref[1:2] = shift_sum
        sums_ref[2:3] = bias_sum
        split_cores(tn(ctx_ref[...], attended_ref[...]), place_ref, keep_ref, send_ref)


def feed_back(place, chips, branch, slope, low, down, down_block, up, outer, unit1, scale1, out_w, vec, ctx):
    rows, width = branch.shape
    hidden = slope.shape[1]
    steps = hidden // width
    whole = full((rows, width))
    end = steps - 1
    part = width // (2 * chips)
    return pl.pallas_call(
        feed_back_kernel,
        grid=(steps + 1,),
        in_specs=[
            pl.BlockSpec(memory_space=pltpu.SMEM),
            whole,
            pl.BlockSpec((rows, width), lambda i: (0, jnp.minimum(i, end))),
            full((width, rows)),
            pl.BlockSpec(down_block, lambda i: (jnp.minimum(i, end), 0, 0)),
            pl.BlockSpec((1, width, width), lambda i: (jnp.minimum(i, end), 0, 0)),
            whole,
            whole,
            full((rows, 1)),
            pl.BlockSpec((1, width, width), lambda i: (3, 0, 0)),
            full(vec.shape),
            whole,
        ],
        out_specs=[
            pl.BlockSpec((chips, part, width), lambda i: (0, 0, i)),
            pl.BlockSpec((chips, part, width), lambda i: (0, 0, i)),
            pl.BlockSpec((1, width), lambda i: (0, jnp.minimum(i, end))),
            whole,
            whole,
            whole,
            full((3, width)),
        ],
        out_shape=[
            jax.ShapeDtypeStruct((chips, part, hidden + width), BF),
            jax.ShapeDtypeStruct((chips, part, hidden + width), BF),
            jax.ShapeDtypeStruct((1, hidden), F32),
            jax.ShapeDtypeStruct((rows, width), F32),
            jax.ShapeDtypeStruct((rows, width), BF),
            jax.ShapeDtypeStruct((rows, width), BF),
            jax.ShapeDtypeStruct((3, width), F32),
        ],
        scratch_shapes=[pltpu.VMEM((rows, width), F32), pltpu.VMEM((rows, width), BF)],
        compiler_params=params(),
        cost_estimate=cost(28 * rows * width * width, 40 * rows * width),
        name="feed_back",
    )(place, branch, slope, low, down, up, outer, unit1, scale1, out_w, vec, ctx)


def attend_back_kernel(length, joined_ref, probs_ref, ctx_grad_ref, grad_ref, sum_ref):
    rows, width = ctx_grad_ref.shape
    pairs = width // PAIR

    def one(seq, carry):
        at = pl.ds(pl.multiple_of(seq * length, length), length)

        def columns(part, pair):
            return slice(part * width + pair * PAIR, part * width + (pair + 1) * PAIR)

        prob_grads = []
        for pair in range(pairs):
            vals = split_heads(joined_ref[at, columns(2, pair)])
            prob_grads.append(nt(vals, ctx_grad_ref[at, columns(0, pair)]))
        score_grads = []
        for pair in range(pairs):
            probs = probs_ref[seq, pair]
            halves = []
            for head in range(2):
                cut = slice(head * length, (head + 1) * length)
                held = probs[cut].astype(F32)
                part = prob_grads[pair][cut]
                base = jnp.sum(part * held, axis=0, keepdims=True)
                halves.append((held * (part - base)).astype(BF))
            score_grads.append(halves)
        for pair in range(pairs):
            probs = probs_ref[seq, pair]
            beside = jnp.concatenate([probs[:length], probs[length:]], axis=1)
            ctx_grads = split_heads(ctx_grad_ref[at, columns(0, pair)])
            grad_ref[at, columns(2, pair)] = nn(beside, ctx_grads).astype(BF)
        for pair in range(pairs):
            queries = split_heads(joined_ref[at, columns(0, pair)] * jnp.asarray(0.125, BF))
            beside = jnp.concatenate(score_grads[pair], axis=1)
            grad_ref[at, columns(1, pair)] = nn(beside, queries).astype(BF)
        for pair in range(pairs):
            keys = split_heads(joined_ref[at, columns(1, pair)])
            stacked = jnp.concatenate(score_grads[pair], axis=0)
            grad_ref[at, columns(0, pair)] = (tn(stacked, keys) * 0.125).astype(BF)
        return carry

    lax.fori_loop(0, rows // length, one, 0)
    total = jnp.zeros(sum_ref.shape, F32)
    for m in range(rows // length):
        total += jnp.sum(
            grad_ref[m * length : (m + 1) * length].astype(F32), axis=0, keepdims=True
        )

    @pl.when(pl.program_id(0) == 0)
    def _():
        sum_ref[...] = total

    @pl.when(pl.program_id(0) > 0)
    def _():
        sum_ref[...] += total


def attend_back(joined, probs, ctx_grad, length):
    rows, width = ctx_grad.shape
    count = rows // length
    steps = 2
    block = rows // steps
    pairs = width // PAIR
    return pl.pallas_call(
        functools.partial(attend_back_kernel, length),
        grid=(steps,),
        in_specs=[
            pl.BlockSpec((block, 3 * width), lambda i: (i, 0)),
            pl.BlockSpec((count // steps, pairs, 2 * length, length), lambda i: (i, 0, 0, 0)),
            pl.BlockSpec((block, width), lambda i: (i, 0)),
        ],
        out_specs=[
            pl.BlockSpec((block, 3 * width), lambda i: (i, 0)),
            full((1, 3 * width)),
        ],
        out_shape=[
            jax.ShapeDtypeStruct((rows, 3 * width), BF),
            jax.ShapeDtypeStruct((1, 3 * width), F32),
        ],
        compiler_params=params(),
        cost_estimate=cost(rows * width, rows * width),
        name="attend_back",
    )(joined, probs, ctx_grad)


def weight_grads_kernel(
    place_ref, tok_ref, joined_ref, small_ref, keep_ref, send_ref, turned_ref
):
    chips, part, _ = keep_ref.shape
    step = pl.program_id(0)
    width = tok_ref.shape[1]
    first = place_ref[2] == 0

    @pl.when(step == 0)
    def _():
        turned_ref[...] = tok_ref[...].T

    value = nn(turned_ref[...], joined_ref[...])
    cols = pl.ds(pl.multiple_of(step * width, width), width)
    for chip in range(chips):
        even = value[2 * chip * part : (2 * chip + 1) * part]
        odd = value[(2 * chip + 1) * part : (2 * chip + 2) * part]
        keep_ref[chip, :, cols] = jnp.where(first, even, odd).astype(BF)
        send_ref[chip, :, cols] = jnp.where(first, odd, even).astype(BF)

    lines = small_ref.shape[1]
    if keep_ref.shape[2] > 3 * width:

        @pl.when(step == 0)
        def _():
            tail = slice(3 * width, keep_ref.shape[2])
            keep_ref[:, :, tail] = jnp.zeros((chips, part, keep_ref.shape[2] - 3 * width), BF)
            send_ref[:, :, tail] = jnp.zeros((chips, part, keep_ref.shape[2] - 3 * width), BF)
            for chip in range(chips):
                even, odd = small_ref[2 * chip], small_ref[2 * chip + 1]
                keep_ref[chip, 0:lines, tail] = jnp.where(first, even, odd).astype(BF)
                send_ref[chip, 0:lines, tail] = jnp.where(first, odd, even).astype(BF)


def weight_grads(place, tokens, joined_grad, small, chips, extra):
    rows, width = tokens.shape
    shape = (chips, width // (2 * chips), 3 * width + extra)
    return pl.pallas_call(
        weight_grads_kernel,
        grid=(3,),
        in_specs=[
            pl.BlockSpec(memory_space=pltpu.SMEM),
            full((rows, width)),
            pl.BlockSpec((rows, width), lambda i: (0, i)),
            full(small.shape),
        ],
        out_specs=[full(shape), full(shape)],
        out_shape=[jax.ShapeDtypeStruct(shape, BF)] * 2,
        scratch_shapes=[pltpu.VMEM((width, rows), BF)],
        compiler_params=params(),
        cost_estimate=cost(rows * width, rows * width),
        name="weight_grads",
    )(place, tokens, joined_grad, small)


def input_kernel(inner_ref, joined_ref, w_ref, out_ref):
    width = inner_ref.shape[1]
    total = inner_ref[...]
    for part in range(3):
        total += nt(joined_ref[:, part * width : (part + 1) * width], w_ref[part])
    out_ref[...] = total.astype(BF)


def input_back(inner, joined_grad, qkv):
    rows, width = inner.shape
    steps = 4
    block = rows // steps
    return pl.pallas_call(
        input_kernel,
        grid=(steps,),
        in_specs=[
            pl.BlockSpec((block, width), lambda i: (i, 0)),
            pl.BlockSpec((block, 3 * width), lambda i: (i, 0)),
            full((3, width, width)),
        ],
        out_specs=pl.BlockSpec((block, width), lambda i: (i, 0)),
        out_shape=jax.ShapeDtypeStruct((rows, width), BF),
        compiler_params=params(),
        cost_estimate=cost(rows * width, rows * width),
        name="input_back",
    )(inner, joined_grad, qkv)


def lay_kernel(plan, chips, reps, part, counts, place_ref, *refs):
    at = 0
    groups = []
    for number in counts:
        groups.append(refs[at : at + number])
        at += number
    sems = refs[-1]
    rep, chip, core = place_ref[0], place_ref[1], place_ref[2]
    copies = []

    def start(source, target):
        copies.append(pltpu.make_async_copy(source, target, sems.at[len(copies)]))
        copies[-1].start()

    finish = plan(start, groups, refs[at:-1], rep, chip, core, chips, reps, part)
    for copy in copies:
        copy.wait()
    if finish is not None:
        finish()


def blocks_plan(
    put, own, twin, along, across, swapped, depth, first, rep, chip, core, chips, reps, part
):
    for block in range(reps):
        put(own(block), block, chip, core)
        put(twin(block), block, chip, 1 - core)
    for step in range(1, chips):
        source = lax.rem(chip + chips - step, chips)
        rows = pl.ds((step - 1) * depth + first, part)
        for other, block in along.items():
            put(block(step, source, 0), rep ^ other, source, core)
            put(block(step, source, 1), rep ^ other, source, 1 - core)
        for other in across:
            put(across[other].at[rows], rep ^ other, source, core)
            put(swapped[other].at[rows], rep ^ other, source, 1 - core)


def wide_put(start, out_ref, part):
    def put(source, block, at_chip, at_core):
        row = pl.multiple_of((at_chip * 2 + at_core) * part, part)
        start(source, out_ref.at[block, pl.ds(row, part)])

    return put


def wide_block(ref, width, part):
    return lambda block: ref.at[pl.ds(0, part), pl.ds(block * width, width)]


def first_plan(start, groups, outs, rep, chip, core, chips, reps, part):
    (own, twin), along, across, swapped, (extra,) = groups
    out_ref, vec_ref, more_ref = outs
    width = out_ref.shape[2]

    def near(step, source, side):
        if side == 0:
            return along[step - 1].at[pl.ds(0, part)]
        return swapped[0].at[pl.ds((step - 1) * part, part)]

    blocks_plan(
        wide_put(start, out_ref, part),
        wide_block(own, width, part),
        wide_block(twin, width, part),
        {0: near},
        {at + 1: ref for at, ref in enumerate(across)},
        {at + 1: ref for at, ref in enumerate(swapped[1:])},
        part,
        0,
        rep,
        chip,
        core,
        chips,
        reps,
        part,
    )
    tail = pl.ds(part, 16)
    cols = pl.ds(0, width)
    start(own.at[tail, cols], more_ref.at[chip * 2 + core])
    start(twin.at[tail, cols], more_ref.at[chip * 2 + 1 - core])
    for step in range(1, chips):
        source = lax.rem(chip + chips - step, chips)
        start(along[step - 1].at[tail], more_ref.at[source * 2 + core])
        start(extra.at[pl.ds((step - 1) * 16, 16)], more_ref.at[source * 2 + 1 - core])

    def finish():
        lane = lax.broadcasted_iota(jnp.int32, (LANES, width), 0)
        place = lax.broadcasted_iota(jnp.int32, (LANES, width), 1)
        total = jnp.zeros((16, width), F32)
        for shard in range(2 * chips):
            there = (place - shard * part == lane) & (lane < part)
            total += nn(more_ref[shard, :, 0:LANES], there.astype(F32).astype(BF))
        vec_ref[...] = total

    return finish


def second_plan(start, groups, outs, rep, chip, core, chips, reps, part):
    (up, up_twin, down, down_twin), (close, far), across, swapped = groups
    up_ref, down_ref = outs
    width = up_ref.shape[2]
    where = (rep, chip, core, chips, reps, part)

    def chained(chain, first):
        def block(step, source, side):
            shard = source * 2 + (core if side == 0 else 1 - core)
            return chain.at[shard, pl.ds(first, part)]

        return block

    across = dict(zip(NEAR, across))
    swapped = dict(zip(NEAR, swapped))
    blocks_plan(
        wide_put(start, up_ref, part),
        wide_block(up, width, part),
        wide_block(up_twin, width, part),
        {0: chained(close, 0), FAR: chained(far, 0)},
        across,
        swapped,
        2 * part,
        0,
        *where,
    )

    def put(source, block, at_chip, at_core):
        row = pl.multiple_of(block * part, part)
        start(source, down_ref.at[at_chip * 2 + at_core, pl.ds(row, part)])

    def tall(ref):
        return lambda block: ref.at[pl.ds(block * part, part)]

    blocks_plan(
        put,
        tall(down),
        tall(down_twin),
        {0: chained(close, part), FAR: chained(far, part)},
        across,
        swapped,
        2 * part,
        part,
        *where,
    )


def lay(plan, place, groups, shapes, scratch, copies, part, chips, reps):
    anywhere = pl.BlockSpec(memory_space=pl.ANY)
    inputs = [ref for group in groups for ref in group]
    return pl.pallas_call(
        functools.partial(
            lay_kernel, plan, chips, reps, part, [len(group) for group in groups]
        ),
        in_specs=[pl.BlockSpec(memory_space=pltpu.SMEM)] + [anywhere] * len(inputs),
        out_specs=[pl.BlockSpec(memory_space=pltpu.VMEM)] * len(shapes),
        out_shape=[jax.ShapeDtypeStruct(shape, kind) for shape, kind in shapes],
        scratch_shapes=[pltpu.VMEM(shape, BF) for shape in scratch]
        + [pltpu.SemaphoreType.DMA((copies,))],
        compiler_params=pltpu.CompilerParams(vmem_limit_bytes=VMEM_BYTES),
        cost_estimate=cost(0, 4 * sum(math.prod(shape) for shape, kind in shapes)),
        name="lay",
    )(place, *inputs)


def pack_vectors(rows, up_bias, class_weight):
    part = rows[0].shape[0]
    lines = [row[None] for row in rows[:8]] + [class_weight.T] + [row[None] for row in rows[8:]]
    pieces = up_bias.shape[0] // part
    lines += [up_bias[None, at * part : (at + 1) * part] for at in range(pieces)]
    return jnp.concatenate(lines, axis=0)


def move(values, reps, chips, target):
    pairs = []
    for rep in range(reps):
        for chip in range(chips):
            for core in range(2):
                to_rep, to_chip, to_core = target(rep, chip, core)
                pairs.append(
                    (
                        (rep * chips + chip) * 2 + core,
                        (to_rep * chips + to_chip) * 2 + to_core,
                    )
                )
    return lax.ppermute(values, ("rep", "fsdp"), pairs)


def along_chips(step, chips):
    return lambda rep, chip, core: (rep, (chip + step) % chips, core)


def across_reps(other):
    return lambda rep, chip, core: (rep ^ other, chip, core)


def to_twin(rep, chip, core):
    return rep, chip, 1 - core


def after(values, *gates):
    return lax.optimization_barrier((values, *gates))[0]


def along_z(mine, reps, chips):
    return [move(mine, reps, chips, along_chips(step, chips)) for step in range(1, chips)]


def over_reps(stacked, reps, chips, others):
    return [move(stacked, reps, chips, across_reps(other)) for other in others]


def pick(parts, at):
    return lax.dynamic_index_in_dim(parts, at, axis=0, keepdims=False)


def in_order(rep, reps, own, others, axis):
    blocks = jnp.stack([own] + others)
    return jnp.concatenate([pick(blocks, rep ^ at) for at in range(reps)], axis=axis)


class Reduction:
    def __init__(self, place, keep, send, reps, chips):
        self.rep, self.chip = place[0], place[1]
        self.reps, self.chips = reps, chips
        self.keep = keep
        self.got = move(send, reps, chips, to_twin)

    def at_rep(self, at):
        return lax.dynamic_index_in_dim(self.both, at, axis=1, keepdims=False)

    def over_reps(self):
        chips, rows, width = self.keep.shape
        both = (self.keep.astype(F32) + self.got.astype(F32)).astype(BF)
        self.both = lax.optimization_barrier(both).reshape(
            chips, self.reps, rows // self.reps, width
        )
        self.arrived = [self.over_rep(other) for other in NEAR]

    def over_rep(self, other, *gates):
        block = self.at_rep(self.rep ^ other)
        if gates:
            block = after(block, *gates)
        return move(block, self.reps, self.chips, across_reps(other))

    def over_far(self, *gates):
        self.arrived = self.arrived + [self.over_rep(FAR, *gates)]

    def over_chips(self, *gates):
        if gates:
            self.arrived = [after(block, *gates) for block in self.arrived]
        total = self.at_rep(self.rep).astype(F32)
        for block in self.arrived:
            total = total + block.astype(F32)
        self.total = pick(total, self.chip)
        self.passed = [
            move(
                pick(total, lax.rem(self.chip + step, self.chips)).astype(BF),
                self.reps,
                self.chips,
                along_chips(step, self.chips),
            )
            for step in range(1, self.chips)
        ]

    def chip_sum(self):
        total = self.total
        for block in self.passed:
            total = total + block.astype(F32)
        return total.astype(BF)


def share_reps(place, total, reps, chips):
    others = [move(total, reps, chips, across_reps(other)) for other in range(1, reps)]
    return in_order(place[0], reps, total, others, 0).astype(F32), others


def exchange_reps(place, rows, reps, chips):
    rep = place[0]
    parts = rows.reshape(reps, -1, rows.shape[1])
    total = pick(parts, rep).astype(F32)
    arrived = [
        move(pick(parts, rep ^ other), reps, chips, across_reps(other))
        for other in range(1, reps)
    ]
    for block in arrived:
        total = total + block.astype(F32)
    return total.astype(BF), arrived


def per_device(
    tokens,
    exit_layer,
    qkv_weight,
    query_bias,
    value_bias,
    out_weight,
    out_bias,
    attn_gain,
    attn_shift,
    up_weight,
    up_bias,
    down_weight,
    down_bias,
    block_gain,
    block_shift,
    pool_weight,
    pool_bias,
    class_weight,
    class_bias,
    output_grad,
    logit_grad,
):
    reps = lax.axis_size("rep")
    shards = lax.axis_size("fsdp")
    mine = lax.axis_index("fsdp")
    rows, width = tokens.shape
    count = exit_layer.shape[0]
    length = rows // count
    classes = class_weight.shape[1]
    part = out_weight.shape[0]
    hidden = up_weight.shape[1]

    def gather(shard):
        return lax.all_gather(shard, "fsdp", axis=0, tiled=True)

    packed = pack_vectors(
        [
            query_bias,
            value_bias,
            out_bias,
            attn_gain,
            attn_shift,
            down_bias,
            block_gain,
            block_shift,
            pool_bias,
        ],
        up_bias,
        class_weight,
    )
    joint_own = jnp.concatenate([qkv_weight, out_weight], axis=1)
    deep = down_weight.shape[0]
    chips = shards // 2
    place = jnp.stack([lax.axis_index("rep"), mine // 2, mine % 2]).astype(jnp.int32)
    direct = (
        part % 16 == 0
        and reps & (reps - 1) == 0
        and reps * width == hidden
        and reps == 4
        and packed.shape[0] <= 16
    )
    if direct:
        lines = packed.shape[0]
        held = jnp.pad(packed, ((0, 16 - lines), (0, width - part)))
        own = jnp.concatenate([joint_own, jnp.tile(held, (1, reps))], axis=0)
        rep = place[0]

        def block_of(weights, at):
            return lax.dynamic_slice_in_dim(weights, at * width, width, axis=1)

        def second_of(at):
            return [
                block_of(up_weight, at),
                lax.dynamic_slice_in_dim(down_weight, at * part, part, axis=0),
            ]

        along = along_z(block_of(own, rep), reps, chips)
        chain = gather(after(jnp.concatenate(second_of(rep), axis=0), *along))
        chain = chain.reshape(chips, 2, 2 * part, width)
        twin = move(own, reps, chips, to_twin)
        stacked = jnp.concatenate([rows_[:part] for rows_ in along], axis=0)
        across = over_reps(stacked, reps, chips, range(1, reps))
        far_chain = gather(after(jnp.concatenate(second_of(rep ^ FAR), axis=0), *across))
        swapped = [move(rows_, reps, chips, to_twin) for rows_ in [stacked] + across]
        extra = move(
            jnp.concatenate([rows_[part:] for rows_ in along], axis=0), reps, chips, to_twin
        )
        up_twin = move(up_weight, reps, chips, to_twin)
        down_twin = move(down_weight, reps, chips, to_twin)
        joint, vec = lay(
            first_plan,
            place,
            [
                [own, twin],
                along,
                across,
                swapped,
                [extra],
            ],
            [((reps, width, width), BF), ((16, width), F32)],
            [(shards, 16, width)],
            2 * chips * (reps + 1),
            part,
            chips,
            reps,
        )
        mine_chain = lax.dynamic_index_in_dim(
            after(chain, joint), place[2], axis=1, keepdims=False
        )
        second_stacked = jnp.concatenate(
            [
                pick(mine_chain, lax.rem(place[1] + chips - step, chips))
                for step in range(1, chips)
            ],
            axis=0,
        )
        second_across = over_reps(after(second_stacked, *across), reps, chips, NEAR)
        up_row = (
            vec[VECTOR_ROWS:lines].reshape(-1, shards, part).transpose(1, 0, 2).reshape(1, hidden)
        )
        down_block = (width // deep, deep, width)
    else:
        small = gather(packed[None])
        vec = small[:, :VECTOR_ROWS].transpose(1, 0, 2).reshape(VECTOR_ROWS, width).astype(F32)
        vec = jnp.pad(vec, ((0, 16 - VECTOR_ROWS), (0, 0)))
        up_row = small[:, VECTOR_ROWS:].transpose(0, 1, 2).reshape(1, hidden).astype(F32)
        pool = gather(pool_weight)
        joint = jnp.stack(jnp.split(gather(joint_own), 4, axis=1))
        up = jnp.stack(jnp.split(gather(up_weight), hidden // width, axis=1))
        down = gather(down_weight).reshape(-1, width, width)
        down_block = (1, width, width)
    joined, probs, ctx = attend(tokens, joint, vec, length)
    if direct:
        pool = gather(after(pool_weight, ctx))
        far_chain = after(far_chain, ctx)
        second_swapped = [
            move(after(rows_, ctx), reps, chips, to_twin) for rows_ in second_across
        ]
        groups = [
            [up_weight, up_twin, down_weight, down_twin],
            [
                chain.reshape(shards, 2 * part, width),
                far_chain.reshape(shards, 2 * part, width),
            ],
            second_across,
            second_swapped,
        ]
        weights = [ref for group in groups for ref in group]
        load = functools.partial(load_second, [len(group) for group in groups], chips, reps, part)
        shapes = [(reps, width, width), (shards, deep, width)]
    else:
        weights, load, shapes = [up, down], None, None
    turned, act, slope, unit1, scale1, unit2, scale2, output, *laid = feed(
        place, exit_layer, tokens, ctx, joint, vec, up_row, weights, load, shapes, length
    )
    if direct:
        up, down = laid
    class_bias_row = jnp.pad(class_bias.astype(F32), (0, 8 - classes))[None]
    logit_grad_rows = jnp.pad(logit_grad, ((0, 0), (0, 8 - classes)))
    outer, branch, low_grad, exit_sums, class_grad, logits, stats = leave(
        exit_layer,
        output,
        unit2,
        scale2,
        output_grad,
        pool,
        vec,
        class_bias_row,
        logit_grad_rows,
        act,
        full((width, width)),
        shards,
        length,
        classes,
    )
    def scatter(grad):
        return lax.psum_scatter(grad, "fsdp", scatter_dimension=0, tiled=True)

    low_part = scatter(low_grad.reshape(-1, width))
    up_keep, up_send, up_sum, inner, attended, ctx_grad, feed_sums = feed_back(
        place, chips, branch, slope, turned, down, down_block, up, outer, unit1, scale1, joint, vec, ctx
    )
    if direct:
        up_red = Reduction(place, up_keep, up_send, reps, chips)
        up_red.over_reps()
        ctx_grad = after(ctx_grad, up_red.both)
    joined_grad, joined_sum = attend_back(joined, probs, ctx_grad, length)
    joined_seen = joined_grad
    if direct:
        joined_seen = after(joined_grad, low_part, *up_red.arrived)
    sums = jnp.concatenate(
        [
            joined_sum.reshape(3, width)[::2],
            feed_sums,
            exit_sums,
            class_grad[:classes],
        ],
        axis=0,
    )
    lines = sums.shape[0]
    own_sums = sums.reshape(lines, shards, part).transpose(1, 0, 2).reshape(shards, lines * part)
    own_sums = jnp.concatenate([own_sums, up_sum.reshape(shards, deep)], axis=1)
    used = own_sums.shape[1]
    seqs_total = count * reps * shards
    figures = jnp.concatenate([stats[0, :1], stats[1, :classes]])
    slots = reps * shards * figures.shape[0] * 3
    direct = direct and used + slots <= part * LANES
    small_lines = 16
    if direct:
        high = figures.astype(BF).astype(F32)
        middle = (figures - high).astype(BF).astype(F32)
        lowest = figures - high - middle
        split = jnp.concatenate([high, middle, lowest])
        slot = lax.axis_index("rep") * shards + mine
        lone = jnp.where(
            jnp.arange(reps * shards)[:, None] == slot, split[None], 0.0
        ).reshape(1, slots)
        row = jnp.concatenate([own_sums, jnp.broadcast_to(lone, (shards, slots))], axis=1)
        small_lines = -(-row.shape[1] // (LANES * 16)) * 16
        row = jnp.pad(row, ((0, 0), (0, small_lines * LANES - row.shape[1])))
        row = row.reshape(shards, small_lines, LANES)
    else:
        row = jnp.zeros((shards, small_lines, LANES), F32)
    keep, send = weight_grads(
        place, tokens, joined_seen, row, chips, LANES if direct else 0
    )
    input_grad = input_back(inner, joined_grad, joint)

    if direct:
        up_red.over_far(keep)
        joint_red = Reduction(place, keep, send, reps, chips)
        joint_red.over_reps()
        up_red.over_chips()
        joint_red.over_far()
        low_total, low_arrived = exchange_reps(
            place, after(low_part, *joint_red.arrived), reps, chips
        )
        joint_red.over_chips(*up_red.passed)
        wide = (deep + part) * width // part
        up_total = up_red.chip_sum()
        joint_total = joint_red.chip_sum()
        columns = up_total.shape[1]
        others = columns + joint_total.shape[1]
        total, _ = share_reps(
            place,
            jnp.concatenate([up_total, joint_total, low_total.reshape(-1, wide)], axis=1),
            reps,
            chips,
        )
        up_sum = total[:, :columns]
        joint_sum = total[:, columns:others]
        low_sum = total[:, others:].reshape(deep + part, width)
        small_sum = joint_sum[:small_lines, 3 * width :].reshape(-1)
        total = small_sum[used : used + slots].reshape(-1, figures.shape[0]).sum(axis=0)
    else:
        first = mine % 2 == 0

        def whole_of(kept, sent):
            pair = jnp.stack([jnp.where(first, kept, sent), jnp.where(first, sent, kept)], axis=1)
            return pair.reshape(-1, kept.shape[2])

        joint_sum, low_sum, up_sum = lax.psum(
            (scatter(whole_of(keep, send)), low_part, scatter(whole_of(up_keep, up_send))), "rep"
        )
        joint_sum, low_sum, up_sum = (
            joint_sum.astype(F32),
            low_sum.astype(F32),
            up_sum.astype(F32),
        )
        own_sums, total = lax.psum((own_sums, figures), ("rep", "fsdp"))
        small_sum = pick(own_sums, mine)
    own = small_sum[: lines * part].reshape(lines, part)
    return (
        output,
        logits[:, :classes],
        total[0] / seqs_total,
        input_grad,
        joint_sum[:, : 3 * width],
        own[0],
        own[1],
        up_sum[:, hidden:],
        own[4],
        own[2],
        own[3],
        up_sum[:, :hidden],
        small_sum[lines * part : used],
        low_sum[:deep],
        own[7],
        own[5],
        own[6],
        low_sum[deep:],
        own[8],
        own[9 : 9 + classes].T,
        total[1:],
    )


def solution(mesh):
    return jax.shard_map(
        per_device,
        mesh=mesh,
        in_specs=(
            P(("rep", "fsdp"), None),
            P(("rep", "fsdp")),
            P("fsdp", None),
            P("fsdp"),
            P("fsdp"),
            P("fsdp", None),
            P("fsdp"),
            P("fsdp"),
            P("fsdp"),
            P("fsdp", None),
            P("fsdp"),
            P("fsdp", None),
            P("fsdp"),
            P("fsdp"),
            P("fsdp"),
            P("fsdp", None),
            P("fsdp"),
            P("fsdp", None),
            P(),
            P(("rep", "fsdp"), None),
            P(("rep", "fsdp"), None),
        ),
        out_specs=(
            P(("rep", "fsdp"), None),
            P(("rep", "fsdp"), None),
            P(),
            P(("rep", "fsdp"), None),
            P("fsdp", None),
            P("fsdp"),
            P("fsdp"),
            P("fsdp", None),
            P("fsdp"),
            P("fsdp"),
            P("fsdp"),
            P("fsdp", None),
            P("fsdp"),
            P("fsdp", None),
            P("fsdp"),
            P("fsdp"),
            P("fsdp"),
            P("fsdp", None),
            P("fsdp"),
            P("fsdp", None),
            P(),
        ),
        check_vma=False,
    )
```

profile of v0, /device:TPU:0, one launch (start us, length us, event | category | flops | bytes accessed | tf_op | source)
XLA Modules:
  0.0 316.2 jit_solution(4609399084553161654)
XLA Ops:
  10.9 3.1 collective-permute-start.1
  14.0 2.6 collective-permute-start.2
  18.8 2.6 collective-permute-done.1.refs_2_
  21.3 6.5 %collective-permute-done.2.refs_3_ = bf16[112,768]{1,0:T(8,128)(2,1)S(1)} collective-permute-done((bf16[112,768]{1,0:T(8,128)(2,1)S(1)}, bf16[112,768]{1,0:T(8,128)(2,1)S(1)}, u32[]{:S(2)}, u32[]{:S(2)}) %collective-permute-start.2) | collective-permute-done | bytes 172064 | tf_op jit(solution)/shard_map/ppermute | solution.py:1004
  32.4 8.8 %collective-permute-done.4.refs_5_ = bf16[288,768]{1,0:T(8,128)(2,1)S(1)} collective-permute-done((bf16[288,768]{1,0:T(8,128)(2,1)S(1)}, bf16[288,768]{1,0:T(8,128)(2,1)S(1)}, u32[]{:S(2)}, u32[]{:S(2)}) %collective-permute-start.4) | collective-permute-done | bytes 442400 | tf_op jit(solution)/shard_map/ppermute | solution.py:1004
  41.2 9.6 %collective-permute-done.5.refs_6_ = bf16[288,768]{1,0:T(8,128)(2,1)S(1)} collective-permute-done((bf16[288,768]{1,0:T(8,128)(2,1)S(1)}, bf16[288,768]{1,0:T(8,128)(2,1)S(1)}, u32[]{:S(2)}, u32[]{:S(2)}) %collective-permute-start.5) | collective-permute-done | bytes 442400 | tf_op jit(solution)/shard_map/ppermute | solution.py:1004
  56.9 5.7 %lay.1 = (bf16[4,768,768]{2,1,0:T(8,128)(2,1)}, f32[16,768]{1,0:T(8,128)}) custom-call(s32[3]{0:T(128)} %pad_add_fusion.place_ref, bf16[112,3072]{1,0:T(8,128)(2,1)} %copy-done, bf16[112,3072]{1,0:T(8,128)(2,1)} %copy-done.4, bf16[112,768]{1,0:T(8,128)(2,1)} %copy-done.5, bf16[112,768]{1,0:T(8,128)(2,1)} %copy-done.6, bf16[112,768]{1,0:T(8,128)(2,1)} %copy-done.7, ...), custom_call_target="tpu_custom_call" | custom-call | bytes 9486336 | tf_op jit(solution)/shard_map/lay/pallas_call | solution.py:969
  66.9 13.6 %attend.1 = (bf16[1024,2304]{1,0:T(8,128)(2,1)}, bf16[8,6,256,128]{3,2,1,0:T(8,128)(2,1)}, bf16[1024,768]{1,0:T(8,128)(2,1)}) custom-call(bf16[1024,768]{1,0:T(8,128)(2,1)} %tok_ref.5, bf16[4,768,768]{2,1,0:T(8,128)(2,1)} %get-tuple-element.68.w_ref.out_w_ref, f32[16,768]{1,0:T(8,128)} %get-tuple-element.69.vec_ref), custom_call_target="tpu_custom_call" | custom-call | flops 4831838208 | bytes 15728640 | tf_op jit(solution)/shard_map/attend/pallas_call | solution.py:134
  80.5 5.2 %collective-permute-done.14.refs_6_ = bf16[576,768]{1,0:T(8,128)(2,1)S(1)} collective-permute-done((bf16[576,768]{1,0:T(8,128)(2,1)S(1)}, bf16[576,768]{1,0:T(8,128)(2,1)S(1)}, u32[]{:S(2)}, u32[]{:S(2)}) %collective-permute-start.14) | collective-permute-done | bytes 884768 | tf_op jit(solution)/shard_map/ppermute | solution.py:1004
  90.3 5.2 %all-gather.6.cloned.1.call-done = bf16[1536,768]{1,0:T(8,128)(2,1)} async-done(((bf16[192,768]{1,0:T(8,128)(2,1)}), bf16[1536,768]{1,0:T(8,128)(2,1)}) %all-gather.6.cloned.1.call-update) | async-done | bytes 2359312 | tf_op jit(solution)/shard_map/all_gather | solution.py:1143
  96.6 29.5 %feed.1 = (bf16[768,1024]{1,0:T(8,128)(2,1)}, bf16[3072,1024]{1,0:T(8,128)(2,1)}, bf16[1024,3072]{1,0:T(8,128)(2,1)}, bf16[1024,768]{1,0:T(8,128)(2,1)}, f32[102...) custom-call(s32[3]{0:T(128)} %pad_add_fusion.place_ref, ...), custom_call_target="tpu_custom_call" | custom-call | flops 10871635968 | bytes 31457280 | tf_op jit(solution)/shard_map/feed/pallas_call | solution.py:300
  126.1 15.3 %leave.1 = (f32[1024,768]{1,0:T(8,128)}, bf16[1024,768]{1,0:T(8,128)(2,1)}, bf16[8,480,768]{2,1,0:T(8,128)(2,1)}, f32[4,768]{1,0:T(4,128)}, f32[8,768]{1,0:T(8,128)}, /*index=5*/f32[8,8]{1,0:T(8,128)}, f32[2,8]{1,0:T(2,128)}) custom-call(s32[8]{0:T(128)} %exit_ref.3, bf16[1024,768]{1,0:T(8,128)(2,1)} %get-tuple-element.136.output_ref, ...), custom_call_target="tpu_custom_call" | custom-call | flops 4831838208 | bytes 23592960 | tf_op jit(solution)/shard_map/leave/pallas_call | solution.py:478
  141.5 29.7 %feed_back.1 = (bf16[4,96,3840]{2,1,0:T(8,128)(2,1)}, bf16[4,96,3840]{2,1,0:T(8,128)(2,1)}, f32[1,3072]{1,0:T(1,128)}, f32[1024,768]{1,0:T(8,128)}, bf16[1024,76...) custom-call(s32[3]{0:T(128)} %pad_add_fusion.place_ref, ...), custom_call_target="tpu_custom_call" | custom-call | flops 16911433728 | bytes 31457280 | tf_op jit(solution)/shard_map/feed_back/pallas_call | solution.py:613
  172.8 4.3 %collective-permute-done.18 = bf16[4,96,3840]{2,1,0:T(8,128)(2,1)S(1)} collective-permute-done((bf16[4,96,3840]{2,1,0:T(8,128)(2,1)}, bf16[4,96,3840]{2,1,0:T(8,128)(2,1)S(1)}, u32[]{:S(2)}, u32[]{:S(2)}) %collective-permute-start.18) | collective-permute-done | bytes 2949152 | tf_op jit(solution)/shard_map/ppermute | solution.py:1004
  178.7 3.4 %add_convert_fusion = bf16[4,96,3840]{2,1,0:T(8,128)(2,1)S(1)} fusion(bf16[4,96,3840]{2,1,0:T(8,128)(2,1)} %copy-done.1, bf16[4,96,3840]{2,1,0:T(8,128)(2,1)} %get-tuple-element.92), kind=kLoop, calls=%fused_computation | loop fusion | flops 5898240 | bytes 8847360 | tf_op jit(solution)/shard_map/convert_element_type | solution.py:1052
  187.6 10.4 %attend_back.1 = (bf16[1024,2304]{1,0:T(8,128)(2,1)}, f32[1,2304]{1,0:T(1,128)}) custom-call(bf16[1024,2304]{1,0:T(8,128)(2,1)} %get-tuple-element.94.joined_ref, bf16[8,6,256,128]{3,2,1,0:T(8,128)(2,1)} %get-tuple-element.95.probs_ref, bf16[1024,768]{1,0:T(8,128)(2,1)} %get-tuple-element.97.ctx_grad_ref), custom_call_target="tpu_custom_call" | custom-call | flops 786432 | bytes 786432 | tf_op jit(solution)/shard_map/attend_back/pallas_call | solution.py:717
  199.7 2.7 collective-permute-done.19
  203.3 3.5 %reduce-scatter.2.cloned.1.call-done = bf16[480,768]{1,0:T(8,128)(2,1)} async-done(((bf16[3840,768]{1,0:T(8,128)(2,1)}), bf16[480,768]{1,0:T(8,128)(2,1)}) %reduce-scatter.2.cloned.1.call-update) | async-done | bytes 737296 | tf_op jit(solution)/shard_map/reduce_scatter | solution.py:1286
  206.9 8.6 %weight_grads.1 = (bf16[4,96,2432]{2,1,0:T(8,128)(2,1)}, bf16[4,96,2432]{2,1,0:T(8,128)(2,1)}) custom-call(s32[3]{0:T(128)} %pad_add_fusion.place_ref, bf16[1024,768]{1,0:T(8,128)(2,1)} %tok_ref.5, bf16[1024,2304]{1,0:T(8,128)(2,1)} %get-tuple-element.100.joined_ref, f32[8,16,128]{2,1,0:T(8,128)} %bitcast.160), custom_call_target="tpu_custom_call" | custom-call | flops 786432 | bytes 786432 | tf_op jit(solution)/shard_map/weight_grads/pallas_call | solution.py:776
  215.5 2.4 collective-permute-start.21
  217.9 14.9 %collective-permute-done.21 = bf16[4,24,3840]{2,1,0:T(8,128)(2,1)} collective-permute-done((bf16[4,24,3840]{2,1,0:T(8,128)(2,1)}, bf16[4,24,3840]{2,1,0:T(8,128)(2,1)}, u32[]{:S(2)}, u32[]{:S(2)}) %collective-permute-start.21) | collective-permute-done | bytes 737312 | tf_op jit(solution)/shard_map/ppermute | solution.py:1004
  232.8 1.9 fusion.1
  234.8 1.7 collective-permute-start.22
  238.0 2.6 collective-permute-start.24
  240.6 2.0 add_convert_fusion.1
  246.3 3.9 %collective-permute-done.23 = bf16[24,3840]{1,0:T(8,128)(2,1)S(1)} collective-permute-done((bf16[24,3840]{1,0:T(8,128)(2,1)S(1)}, bf16[24,3840]{1,0:T(8,128)(2,1)S(1)}, u32[]{:S(2)}, u32[]{:S(2)}) %collective-permute-start.23) | collective-permute-done | bytes 184352 | tf_op jit(solution)/shard_map/ppermute | solution.py:1004
  250.3 6.2 %collective-permute-done.26 = bf16[4,24,2432]{2,1,0:T(8,128)(2,1)S(1)} collective-permute-done((bf16[4,24,2432]{2,1,0:T(8,128)(2,1)S(1)}, bf16[4,24,2432]{2,1,0:T(8,128)(2,1)S(1)}, u32[]{:S(2)}, u32[]{:S(2)}) %collective-permute-start.26) | collective-permute-done | bytes 466976 | tf_op jit(solution)/shard_map/ppermute | solution.py:1004
  256.4 9.3 %collective-permute-done.27 = bf16[4,24,2432]{2,1,0:T(8,128)(2,1)S(1)} collective-permute-done((bf16[4,24,2432]{2,1,0:T(8,128)(2,1)S(1)}, bf16[4,24,2432]{2,1,0:T(8,128)(2,1)S(1)}, u32[]{:S(2)}, u32[]{:S(2)}) %collective-permute-start.27) | collective-permute-done | bytes 466976 | tf_op jit(solution)/shard_map/ppermute | solution.py:1004
  273.5 3.3 %collective-permute-done.30 = bf16[24,2432]{1,0:T(8,128)(2,1)S(1)} collective-permute-done((bf16[24,2432]{1,0:T(8,128)(2,1)S(1)}, bf16[24,2432]{1,0:T(8,128)(2,1)S(1)}, u32[]{:S(2)}, u32[]{:S(2)}) %collective-permute-start.30) | collective-permute-done | bytes 116768 | tf_op jit(solution)/shard_map/ppermute | solution.py:1004
  282.5 8.7 %input_back.1 = bf16[1024,768]{1,0:T(8,128)(2,1)} custom-call(f32[1024,768]{1,0:T(8,128)} %get-tuple-element.114.inner_ref, bf16[1024,2304]{1,0:T(8,128)(2,1)} %get-tuple-element.100.joined_ref, bf16[4,768,768]{2,1,0:T(8,128)(2,1)} %get-tuple-element.68.w_ref.out_w_ref), custom_call_target="tpu_custom_call" | custom-call | flops 786432 | bytes 786432 | tf_op jit(solution)/shard_map/input_back/pallas_call | solution.py:806
  291.2 2.0 collective-permute-done.37
  293.3 6.7 %collective-permute-done.36 = bf16[24,10112]{1,0:T(8,128)(2,1)S(1)} collective-permute-done((bf16[24,10112]{1,0:T(8,128)(2,1)S(1)}, bf16[24,10112]{1,0:T(8,128)(2,1)S(1)}, u32[]{:S(2)}, u32[]{:S(2)}) %collective-permute-start.36) | collective-permute-done | bytes 485408 | tf_op jit(solution)/shard_map/ppermute | solution.py:1004
  (203 shorter events, 64.5 us)
Async XLA Ops:
  7.2 55.4 %all-gather.4.cloned.1.call-start = ((), (), s32[]{:S(2)}) async-start(), calls=%async_computation.1 | async-start | bytes 2654208 | tf_op jit(solution)/shard_map/all_gather | solution.py:1143
  10.9 10.4 %collective-permute-start.1 = (bf16[112,768]{1,0:T(8,128)(2,1)S(1)}, bf16[112,768]{1,0:T(8,128)(2,1)S(1)}, u32[]{:S(2)}, u32[]{:S(2)}) collective-permute-start(bf16[112,768]{1,0:T(8,128)(2,1)S(1)} %constant_dynamic-slice_fusion.4), channel_id=1, source_target_pairs={{0,2},{1,3},{2,4},{3,5},{4,6},{5,7},{6,0},{7,1},{8,10},{9,11},{10,... | collective-permute-start | bytes 516104 | tf_op jit(solution)/shard_map/ppermute | solution.py:1004
  14.0 13.9 %collective-permute-start.2 = (bf16[112,768]{1,0:T(8,128)(2,1)S(1)}, bf16[112,768]{1,0:T(8,128)(2,1)S(1)}, u32[]{:S(2)}, u32[]{:S(2)}) collective-permute-start(bf16[112,768]{1,0:T(8,128)(2,1)S(1)} %constant_dynamic-slice_fusion.4), channel_id=1, source_target_pairs={{0,4},{1,5},{2,6},{3,7},{4,0},{5,1},{6,2},{7,3},{8,12},{9,13},{10,... | collective-permute-start | bytes 516104 | tf_op jit(solution)/shard_map/ppermute | solution.py:1004
  16.6 11.3 %collective-permute-start.3 = (bf16[112,768]{1,0:T(8,128)(2,1)S(1)}, bf16[112,768]{1,0:T(8,128)(2,1)S(1)}, u32[]{:S(2)}, u32[]{:S(2)}) collective-permute-start(bf16[112,768]{1,0:T(8,128)(2,1)S(1)} %constant_dynamic-slice_fusion.4), channel_id=1, source_target_pairs={{0,6},{1,7},{2,0},{3,1},{4,2},{5,3},{6,4},{7,5},{8,14},{9,15},{10,... | collective-permute-start | bytes 516104 | tf_op jit(solution)/shard_map/ppermute | solution.py:1004
  27.9 67.6 %all-gather.6.cloned.1.call-start = ((), (), s32[]{:S(2)}) async-start(), calls=%async_computation.2 | async-start | bytes 2654208 | tf_op jit(solution)/shard_map/all_gather | solution.py:1143
  28.1 13.1 %collective-permute-start.4 = (bf16[288,768]{1,0:T(8,128)(2,1)S(1)}, bf16[288,768]{1,0:T(8,128)(2,1)S(1)}, u32[]{:S(2)}, u32[]{:S(2)}) collective-permute-start(bf16[288,768]{1,0:T(8,128)(2,1)S(1)} %pad_maximum_fusion.4), channel_id=1, source_target_pairs={{0,8},{1,9},{2,10},{3,11},{4,12},{5,13},{6,14},{7,15},{8,0},{9,1},... | collective-permute-start | bytes 1327112 | tf_op jit(solution)/shard_map/ppermute | solution.py:1004
  29.6 21.2 %collective-permute-start.5 = (bf16[288,768]{1,0:T(8,128)(2,1)S(1)}, bf16[288,768]{1,0:T(8,128)(2,1)S(1)}, u32[]{:S(2)}, u32[]{:S(2)}) collective-permute-start(bf16[288,768]{1,0:T(8,128)(2,1)S(1)} %pad_maximum_fusion.4), channel_id=1, source_target_pairs={{0,16},{1,17},{2,18},{3,19},{4,20},{5,21},{6,22},{7,23},{8,24},{9,... | collective-permute-start | bytes 1327112 | tf_op jit(solution)/shard_map/ppermute | solution.py:1004
  31.1 19.7 %collective-permute-start.6 = (bf16[288,768]{1,0:T(8,128)(2,1)S(1)}, bf16[288,768]{1,0:T(8,128)(2,1)S(1)}, u32[]{:S(2)}, u32[]{:S(2)}) collective-permute-start(bf16[288,768]{1,0:T(8,128)(2,1)S(1)} %pad_maximum_fusion.4), channel_id=1, source_target_pairs={{0,24},{1,25},{2,26},{3,27},{4,28},{5,29},{6,30},{7,31},{8,16},{9,... | collective-permute-start | bytes 1327112 | tf_op jit(solution)/shard_map/ppermute | solution.py:1004
  51.6 74.5 %all-gather.8.cloned.1.call-start = ((), (), s32[]{:S(2)}) async-start(), calls=%async_computation.3 | async-start | bytes 1327104 | tf_op jit(solution)/shard_map/all_gather | solution.py:1143
  63.9 21.8 %collective-permute-start.14 = (bf16[576,768]{1,0:T(8,128)(2,1)S(1)}, bf16[576,768]{1,0:T(8,128)(2,1)S(1)}, u32[]{:S(2)}, u32[]{:S(2)}) collective-permute-start(bf16[576,768]{1,0:T(8,128)(2,1)S(1)} %pad_maximum_fusion.1), channel_id=1, source_target_pairs={{0,8},{1,9},{2,10},{3,11},{4,12},{5,13},{6,14},{7,15},{8,0},{9,1},... | collective-permute-start | bytes 2654216 | tf_op jit(solution)/shard_map/ppermute | solution.py:1004
  65.4 21.6 %collective-permute-start.15 = (bf16[576,768]{1,0:T(8,128)(2,1)S(1)}, bf16[576,768]{1,0:T(8,128)(2,1)}, u32[]{:S(2)}, u32[]{:S(2)}) collective-permute-start(bf16[576,768]{1,0:T(8,128)(2,1)S(1)} %pad_maximum_fusion.1), channel_id=1, source_target_pairs={{0,16},{1,17},{2,18},{3,19},{4,20},{5,21},{6,22},{7,23},{8,24},{9,... | collective-permute-start | bytes 2654216 | tf_op jit(solution)/shard_map/ppermute | solution.py:1004
  80.4 126.4 %reduce-scatter.2.cloned.1.call-start = ((), (), s32[]{:S(2)}) async-start(), calls=%async_computation.4 | async-start | bytes 6635520 | tf_op jit(solution)/shard_map/reduce_scatter | solution.py:1286
  85.7 9.9 %collective-permute-start.16 = (bf16[576,768]{1,0:T(8,128)(2,1)S(1)}, bf16[576,768]{1,0:T(8,128)(2,1)}, u32[]{:S(2)}, u32[]{:S(2)}) collective-permute-start(bf16[576,768]{1,0:T(8,128)(2,1)S(1)} %collective-permute-done.14.refs_6_), channel_id=1, source_target_pairs={{0,1},{1,0},{2,3},{3,2},{4,5},{5,4},{6,7},{7,6},{8,9},{9,8},{10,11... | collective-permute-start | bytes 2654216 | tf_op jit(solution)/shard_map/ppermute | solution.py:1004
  87.0 8.6 %collective-permute-start.17 = (bf16[576,768]{1,0:T(8,128)(2,1)}, bf16[576,768]{1,0:T(8,128)(2,1)}, u32[]{:S(2)}, u32[]{:S(2)}) collective-permute-start(bf16[576,768]{1,0:T(8,128)(2,1)} %collective-permute-done.15.refs_7_), channel_id=1, source_target_pairs={{0,1},{1,0},{2,3},{3,2},{4,5},{5,4},{6,7},{7,6},{8,9},{9,8},{10,11... | collective-permute-start | bytes 2654216 | tf_op jit(solution)/shard_map/ppermute | solution.py:1004
  87.0 8.6 %collective-permute-start.12 = (bf16[96,3072]{1,0:T(8,128)(2,1)S(1)}, bf16[96,3072]{1,0:T(8,128)(2,1)S(1)}, u32[]{:S(2)}, u32[]{:S(2)}) collective-permute-start(bf16[96,3072]{1,0:T(8,128)(2,1)S(1)} %copy-done.12), channel_id=1, source_target_pairs={{0,1},{1,0},{2,3},{3,2},{4,5},{5,4},{6,7},{7,6},{8,9},{9,8},{10,11... | collective-permute-start | bytes 1769480 | tf_op jit(solution)/shard_map/ppermute | solution.py:1004
  87.5 8.1 %collective-permute-start.13 = (bf16[384,768]{1,0:T(8,128)(2,1)S(1)}, bf16[384,768]{1,0:T(8,128)(2,1)S(1)}, u32[]{:S(2)}, u32[]{:S(2)}) collective-permute-start(bf16[384,768]{1,0:T(8,128)(2,1)S(1)} %copy-done.14), channel_id=1, source_target_pairs={{0,1},{1,0},{2,3},{3,2},{4,5},{5,4},{6,7},{7,6},{8,9},{9,8},{10,11... | collective-permute-start | bytes 1769480 | tf_op jit(solution)/shard_map/ppermute | solution.py:1004
  183.6 18.8 %collective-permute-start.19 = (bf16[4,24,3840]{2,1,0:T(8,128)(2,1)}, bf16[4,24,3840]{2,1,0:T(8,128)(2,1)}, u32[]{:S(2)}, u32[]{:S(2)}) collective-permute-start(bf16[4,24,3840]{2,1,0:T(8,128)(2,1)} %get-tuple-element.161), channel_id=1, source_target_pairs={{0,8},{1,9},{2,10},{3,11},{4,12},{5,13},{6,14},{7,15},{8,0},{9,1},... | collective-permute-start | bytes 2211848 | tf_op jit(solution)/shard_map/ppermute | solution.py:1004
  184.7 18.7 %collective-permute-start.20 = (bf16[4,24,3840]{2,1,0:T(8,128)(2,1)}, bf16[4,24,3840]{2,1,0:T(8,128)(2,1)}, u32[]{:S(2)}, u32[]{:S(2)}) collective-permute-start(bf16[4,24,3840]{2,1,0:T(8,128)(2,1)} %get-tuple-element.160), channel_id=1, source_target_pairs={{0,16},{1,17},{2,18},{3,19},{4,20},{5,21},{6,22},{7,23},{8,24},{9,... | collective-permute-start | bytes 2211848 | tf_op jit(solution)/shard_map/ppermute | solution.py:1004
  215.5 17.3 %collective-permute-start.21 = (bf16[4,24,3840]{2,1,0:T(8,128)(2,1)}, bf16[4,24,3840]{2,1,0:T(8,128)(2,1)}, u32[]{:S(2)}, u32[]{:S(2)}) collective-permute-start(bf16[4,24,3840]{2,1,0:T(8,128)(2,1)} %get-tuple-element.108), channel_id=1, source_target_pairs={{0,24},{1,25},{2,26},{3,27},{4,28},{5,29},{6,30},{7,31},{8,16},{9,... | collective-permute-start | bytes 2211848 | tf_op jit(solution)/shard_map/ppermute | solution.py:1004
  217.8 22.8 %collective-permute-start.25 = (bf16[4,96,2432]{2,1,0:T(8,128)(2,1)}, bf16[4,96,2432]{2,1,0:T(8,128)(2,1)}, u32[]{:S(2)}, u32[]{:S(2)}) collective-permute-start(bf16[4,96,2432]{2,1,0:T(8,128)(2,1)} %get-tuple-element.109), channel_id=1, source_target_pairs={{0,1},{1,0},{2,3},{3,2},{4,5},{5,4},{6,7},{7,6},{8,9},{9,8},{10,11... | collective-permute-start | bytes 5603336 | tf_op jit(solution)/shard_map/ppermute | solution.py:1004
  234.8 11.0 %collective-permute-start.22 = (bf16[24,3840]{1,0:T(8,128)(2,1)S(1)}, bf16[24,3840]{1,0:T(8,128)(2,1)S(1)}, u32[]{:S(2)}, u32[]{:S(2)}) collective-permute-start(bf16[24,3840]{1,0:T(8,128)(2,1)S(1)} %get-tuple-element.176), channel_id=1, source_target_pairs={{0,2},{1,3},{2,4},{3,5},{4,6},{5,7},{6,0},{7,1},{8,10},{9,11},{10,... | collective-permute-start | bytes 552968 | tf_op jit(solution)/shard_map/ppermute | solution.py:1004
  236.4 13.7 %collective-permute-start.23 = (bf16[24,3840]{1,0:T(8,128)(2,1)S(1)}, bf16[24,3840]{1,0:T(8,128)(2,1)S(1)}, u32[]{:S(2)}, u32[]{:S(2)}) collective-permute-start(bf16[24,3840]{1,0:T(8,128)(2,1)S(1)} %get-tuple-element.175), channel_id=1, source_target_pairs={{0,4},{1,5},{2,6},{3,7},{4,0},{5,1},{6,2},{7,3},{8,12},{9,13},{10,... | collective-permute-start | bytes 552968 | tf_op jit(solution)/shard_map/ppermute | solution.py:1004
  238.0 12.2 %collective-permute-start.24 = (bf16[24,3840]{1,0:T(8,128)(2,1)S(1)}, bf16[24,3840]{1,0:T(8,128)(2,1)S(1)}, u32[]{:S(2)}, u32[]{:S(2)}) collective-permute-start(bf16[24,3840]{1,0:T(8,128)(2,1)S(1)} %get-tuple-element.174), channel_id=1, source_target_pairs={{0,6},{1,7},{2,0},{3,1},{4,2},{5,3},{6,4},{7,5},{8,14},{9,15},{10,... | collective-permute-start | bytes 552968 | tf_op jit(solution)/shard_map/ppermute | solution.py:1004
  242.7 13.7 %collective-permute-start.26 = (bf16[4,24,2432]{2,1,0:T(8,128)(2,1)S(1)}, bf16[4,24,2432]{2,1,0:T(8,128)(2,1)S(1)}, u32[]{:S(2)}, u32[]{:S(2)}) collective-permute-start(bf16[4,24,2432]{2,1,0:T(8,128)(2,1)S(1)} %get-tuple-element.173), channel_id=1, source_target_pairs={{0,8},{1,9},{2,10},{3,11},{4,12},{5,13},{6,14},{7,15},{8,0},{9,1},... | collective-permute-start | bytes 1400840 | tf_op jit(solution)/shard_map/ppermute | solution.py:1004
  244.3 21.4 %collective-permute-start.27 = (bf16[4,24,2432]{2,1,0:T(8,128)(2,1)S(1)}, bf16[4,24,2432]{2,1,0:T(8,128)(2,1)S(1)}, u32[]{:S(2)}, u32[]{:S(2)}) collective-permute-start(bf16[4,24,2432]{2,1,0:T(8,128)(2,1)S(1)} %get-tuple-element.172), channel_id=1, source_target_pairs={{0,16},{1,17},{2,18},{3,19},{4,20},{5,21},{6,22},{7,23},{8,24},{9,... | collective-permute-start | bytes 1400840 | tf_op jit(solution)/shard_map/ppermute | solution.py:1004
  245.8 20.0 %collective-permute-start.28 = (bf16[4,24,2432]{2,1,0:T(8,128)(2,1)S(1)}, bf16[4,24,2432]{2,1,0:T(8,128)(2,1)S(1)}, u32[]{:S(2)}, u32[]{:S(2)}) collective-permute-start(bf16[4,24,2432]{2,1,0:T(8,128)(2,1)S(1)} %get-tuple-element.171), channel_id=1, source_target_pairs={{0,24},{1,25},{2,26},{3,27},{4,28},{5,29},{6,30},{7,31},{8,16},{9,... | collective-permute-start | bytes 1400840 | tf_op jit(solution)/shard_map/ppermute | solution.py:1004
  266.6 10.2 %collective-permute-start.30 = (bf16[24,2432]{1,0:T(8,128)(2,1)S(1)}, bf16[24,2432]{1,0:T(8,128)(2,1)S(1)}, u32[]{:S(2)}, u32[]{:S(2)}) collective-permute-start(bf16[24,2432]{1,0:T(8,128)(2,1)S(1)} %get-tuple-element.179), channel_id=1, source_target_pairs={{0,4},{1,5},{2,6},{3,7},{4,0},{5,1},{6,2},{7,3},{8,12},{9,13},{10,... | collective-permute-start | bytes 350216 | tf_op jit(solution)/shard_map/ppermute | solution.py:1004
  267.0 9.8 %collective-permute-start.29 = (bf16[24,2432]{1,0:T(8,128)(2,1)S(1)}, bf16[24,2432]{1,0:T(8,128)(2,1)S(1)}, u32[]{:S(2)}, u32[]{:S(2)}) collective-permute-start(bf16[24,2432]{1,0:T(8,128)(2,1)S(1)} %get-tuple-element.177), channel_id=1, source_target_pairs={{0,2},{1,3},{2,4},{3,5},{4,6},{5,7},{6,0},{7,1},{8,10},{9,11},{10,... | collective-permute-start | bytes 350216 | tf_op jit(solution)/shard_map/ppermute | solution.py:1004
  268.2 8.7 %collective-permute-start.34 = (bf16[120,768]{1,0:T(8,128)(2,1)S(1)}, bf16[120,768]{1,0:T(8,128)(2,1)S(1)}, u32[]{:S(2)}, u32[]{:S(2)}) collective-permute-start(bf16[120,768]{1,0:T(8,128)(2,1)S(1)} %get-tuple-element.181), channel_id=1, source_target_pairs={{0,24},{1,25},{2,26},{3,27},{4,28},{5,29},{6,30},{7,31},{8,16},{9,... | collective-permute-start | bytes 552968 | tf_op jit(solution)/shard_map/ppermute | solution.py:1004
  278.3 15.0 %collective-permute-start.37 = (bf16[24,10112]{1,0:T(8,128)(2,1)S(1)}, bf16[24,10112]{1,0:T(8,128)(2,1)S(1)}, u32[]{:S(2)}, u32[]{:S(2)}) collective-permute-start(bf16[24,10112]{1,0:T(8,128)(2,1)S(1)} %get-tuple-element.188), channel_id=1, source_target_pairs={{0,24},{1,25},{2,26},{3,27},{4,28},{5,29},{6,30},{7,31},{8,16},{9,... | collective-permute-start | bytes 1456136 | tf_op jit(solution)/shard_map/ppermute | solution.py:1004
  279.8 20.1 %collective-permute-start.36 = (bf16[24,10112]{1,0:T(8,128)(2,1)S(1)}, bf16[24,10112]{1,0:T(8,128)(2,1)S(1)}, u32[]{:S(2)}, u32[]{:S(2)}) collective-permute-start(bf16[24,10112]{1,0:T(8,128)(2,1)S(1)} %get-tuple-element.188), channel_id=1, source_target_pairs={{0,16},{1,17},{2,18},{3,19},{4,20},{5,21},{6,22},{7,23},{8,24},{9,... | collective-permute-start | bytes 1456136 | tf_op jit(solution)/shard_map/ppermute | solution.py:1004
  280.9 19.0 %collective-permute-start.35 = (bf16[24,10112]{1,0:T(8,128)(2,1)S(1)}, bf16[24,10112]{1,0:T(8,128)(2,1)S(1)}, u32[]{:S(2)}, u32[]{:S(2)}) collective-permute-start(bf16[24,10112]{1,0:T(8,128)(2,1)S(1)} %get-tuple-element.188), channel_id=1, source_target_pairs={{0,8},{1,9},{2,10},{3,11},{4,12},{5,13},{6,14},{7,15},{8,0},{9,1},... | collective-permute-start | bytes 1456136 | tf_op jit(solution)/shard_map/ppermute | solution.py:1004
  (37 other events, 439.4 us)
Sparse Core Ops, SparseCore 0:
  28.0 34.4 all-gather.3
  64.8 30.7 all-gather.5
  97.2 21.7 all-gather.7
  141.6 65.2 reduce-scatter.1
where the time goes:
time: 317 us; the launch traced here: 316 us
  Pallas kernels  122 us (38%)
  waiting for transfers between devices  103 us (32%)
  starting transfers between devices  39.6 us (12%)
  local copies, waits for them, and re-layouts  20.4 us (6%)
  other arithmetic  16 us (5%)
  between operations  15.5 us (5%)
    ppermute x38, waiting for transfers between devices, move(): return lax.ppermute(values, ('rep', 'fsdp'), pairs)  94.2 us
    ppermute x38, starting transfers between devices, move(): return lax.ppermute(values, ('rep', 'fsdp'), pairs)  39.5 us
    pallas_call x1, Pallas kernels, feed_back(): pl.pallas_call(feed_back_kernel, grid=(steps + 1,), in_specs=[pl.BlockSpe...  29.7 us
    pallas_call x1, Pallas kernels, feed(): pl.pallas_call(functools.partial(feed_kernel, length, load, len(weights))...  29.5 us
    pallas_call x1, Pallas kernels, leave(): pl.pallas_call(functools.partial(leave_kernel, length, classes), grid=(st...  15.3 us
    pallas_call x1, Pallas kernels, attend(): pl.pallas_call(functools.partial(attend_kernel, length), grid=(steps,), i...  13.6 us
    pallas_call x1, Pallas kernels, attend_back(): pl.pallas_call(functools.partial(attend_back_kernel, length), grid=(steps...  10.4 us
    pallas_call x1, Pallas kernels, input_back(): pl.pallas_call(input_kernel, grid=(steps,), in_specs=[pl.BlockSpec((block...  8.75 us
  transfers between devices with their start and end apart: 42, of which 25 were waited for; matrix products, arithmetic and copies ran while one was open for 6% of the time, Pallas kernels for 31%

commit v1 on v0

--- a/solution.py
+++ b/solution.py
@@ -1339,7 +1339,7 @@
         up_red.over_far(keep)
         joint_red = Reduction(place, keep, send, reps, chips)
         joint_red.over_reps()
-        up_red.over_chips()
+        up_red.over_chips(joint_red.both)
         joint_red.over_far()
         low_total, low_arrived = exchange_reps(
             place, after(low_part, *joint_red.arrived), reps, chips

time: 317 us -> 315 us (level)
  waiting for transfers between devices: 103 us -> 98.9 us
    ppermute x38, waiting for transfers between devices: 94.2 us -> 90.1 us  [move(): return lax.ppermute(values, ('rep', 'fsdp'), pairs)]
where the time goes in v1:
time: 315 us
  Pallas kernels  121 us (38%)
  waiting for transfers between devices  98.9 us (31%)
  starting transfers between devices  41.8 us (13%)
  local copies, waits for them, and re-layouts  20.5 us (7%)
  other arithmetic  16.3 us (5%)
  between operations  15.5 us (5%)
    ppermute x38, waiting for transfers between devices, move(): return lax.ppermute(values, ('rep', 'fsdp'), pairs)  90.1 us
    ppermute x38, starting transfers between devices, move(): return lax.ppermute(values, ('rep', 'fsdp'), pairs)  41.7 us
    pallas_call x1, Pallas kernels, feed_back(): pl.pallas_call(feed_back_kernel, grid=(steps + 1,), in_specs=[pl.BlockSpe...  29.6 us
    pallas_call x1, Pallas kernels, feed(): pl.pallas_call(functools.partial(feed_kernel, length, load, len(weights))...  29.5 us
    pallas_call x1, Pallas kernels, leave(): pl.pallas_call(functools.partial(leave_kernel, length, classes), grid=(st...  15.4 us
    pallas_call x1, Pallas kernels, attend(): pl.pallas_call(functools.partial(attend_kernel, length), grid=(steps,), i...  13.6 us
    pallas_call x1, Pallas kernels, attend_back(): pl.pallas_call(functools.partial(attend_back_kernel, length), grid=(steps...  10.4 us
    pallas_call x1, Pallas kernels, input_back(): pl.pallas_call(input_kernel, grid=(steps,), in_specs=[pl.BlockSpec((block...  8.74 us
  transfers between devices with their start and end apart: 42, of which 25 were waited for; matrix products, arithmetic and copies ran while one was open for 6% of the time, Pallas kernels for 31%

profile of v1, /device:TPU:0, one launch (start us, length us, event | category | flops | bytes accessed | tf_op | source)
XLA Modules:
  0.0 314.6 jit_solution(10765296116749855291)
XLA Ops:
  10.9 3.1 collective-permute-start.1
  14.0 2.6 collective-permute-start.2
  18.8 2.6 collective-permute-done.1.refs_2_
  21.3 6.5 %collective-permute-done.2.refs_3_ = bf16[112,768]{1,0:T(8,128)(2,1)S(1)} collective-permute-done((bf16[112,768]{1,0:T(8,128)(2,1)S(1)}, bf16[112,768]{1,0:T(8,128)(2,1)S(1)}, u32[]{:S(2)}, u32[]{:S(2)}) %collective-permute-start.2) | collective-permute-done | bytes 172064 | tf_op jit(solution)/shard_map/ppermute | solution.py:1004
  32.4 8.8 %collective-permute-done.4.refs_5_ = bf16[288,768]{1,0:T(8,128)(2,1)S(1)} collective-permute-done((bf16[288,768]{1,0:T(8,128)(2,1)S(1)}, bf16[288,768]{1,0:T(8,128)(2,1)S(1)}, u32[]{:S(2)}, u32[]{:S(2)}) %collective-permute-start.4) | collective-permute-done | bytes 442400 | tf_op jit(solution)/shard_map/ppermute | solution.py:1004
  41.2 9.6 %collective-permute-done.5.refs_6_ = bf16[288,768]{1,0:T(8,128)(2,1)S(1)} collective-permute-done((bf16[288,768]{1,0:T(8,128)(2,1)S(1)}, bf16[288,768]{1,0:T(8,128)(2,1)S(1)}, u32[]{:S(2)}, u32[]{:S(2)}) %collective-permute-start.5) | collective-permute-done | bytes 442400 | tf_op jit(solution)/shard_map/ppermute | solution.py:1004
  57.0 5.7 %lay.1 = (bf16[4,768,768]{2,1,0:T(8,128)(2,1)}, f32[16,768]{1,0:T(8,128)}) custom-call(s32[3]{0:T(128)} %pad_add_fusion.place_ref, bf16[112,3072]{1,0:T(8,128)(2,1)} %copy-done, bf16[112,3072]{1,0:T(8,128)(2,1)} %copy-done.3, bf16[112,768]{1,0:T(8,128)(2,1)} %copy-done.4, bf16[112,768]{1,0:T(8,128)(2,1)} %copy-done.5, bf16[112,768]{1,0:T(8,128)(2,1)} %copy-done.6, ...), custom_call_target="tpu_custom_call" | custom-call | bytes 9486336 | tf_op jit(solution)/shard_map/lay/pallas_call | solution.py:969
  66.9 13.6 %attend.1 = (bf16[1024,2304]{1,0:T(8,128)(2,1)}, bf16[8,6,256,128]{3,2,1,0:T(8,128)(2,1)}, bf16[1024,768]{1,0:T(8,128)(2,1)}) custom-call(bf16[1024,768]{1,0:T(8,128)(2,1)} %tok_ref.5, bf16[4,768,768]{2,1,0:T(8,128)(2,1)} %get-tuple-element.71.w_ref.out_w_ref, f32[16,768]{1,0:T(8,128)} %get-tuple-element.72.vec_ref), custom_call_target="tpu_custom_call" | custom-call | flops 4831838208 | bytes 15728640 | tf_op jit(solution)/shard_map/attend/pallas_call | solution.py:134
  80.5 5.2 %collective-permute-done.14.refs_6_ = bf16[576,768]{1,0:T(8,128)(2,1)S(1)} collective-permute-done((bf16[576,768]{1,0:T(8,128)(2,1)S(1)}, bf16[576,768]{1,0:T(8,128)(2,1)S(1)}, u32[]{:S(2)}, u32[]{:S(2)}) %collective-permute-start.14) | collective-permute-done | bytes 884768 | tf_op jit(solution)/shard_map/ppermute | solution.py:1004
  90.3 5.2 %all-gather.6.cloned.1.call-done = bf16[1536,768]{1,0:T(8,128)(2,1)} async-done(((bf16[192,768]{1,0:T(8,128)(2,1)}), bf16[1536,768]{1,0:T(8,128)(2,1)}) %all-gather.6.cloned.1.call-update) | async-done | bytes 2359312 | tf_op jit(solution)/shard_map/all_gather | solution.py:1143
  96.6 29.5 %feed.1 = (bf16[768,1024]{1,0:T(8,128)(2,1)}, bf16[3072,1024]{1,0:T(8,128)(2,1)}, bf16[1024,3072]{1,0:T(8,128)(2,1)}, bf16[1024,768]{1,0:T(8,128)(2,1)}, f32[102...) custom-call(s32[3]{0:T(128)} %pad_add_fusion.place_ref, ...), custom_call_target="tpu_custom_call" | custom-call | flops 10871635968 | bytes 31457280 | tf_op jit(solution)/shard_map/feed/pallas_call | solution.py:300
  126.1 15.4 %leave.1 = (f32[1024,768]{1,0:T(8,128)}, bf16[1024,768]{1,0:T(8,128)(2,1)}, bf16[8,480,768]{2,1,0:T(8,128)(2,1)}, f32[4,768]{1,0:T(4,128)}, f32[8,768]{1,0:T(8,128)}, /*index=5*/f32[8,8]{1,0:T(8,128)}, f32[2,8]{1,0:T(2,128)}) custom-call(s32[8]{0:T(128)} %exit_ref.3, bf16[1024,768]{1,0:T(8,128)(2,1)} %get-tuple-element.142.output_ref, ...), custom_call_target="tpu_custom_call" | custom-call | flops 4831838208 | bytes 23592960 | tf_op jit(solution)/shard_map/leave/pallas_call | solution.py:478
  141.5 29.6 %feed_back.1 = (bf16[4,96,3840]{2,1,0:T(8,128)(2,1)}, bf16[4,96,3840]{2,1,0:T(8,128)(2,1)}, f32[1,3072]{1,0:T(1,128)}, f32[1024,768]{1,0:T(8,128)}, bf16[1024,76...) custom-call(s32[3]{0:T(128)} %pad_add_fusion.place_ref, ...), custom_call_target="tpu_custom_call" | custom-call | flops 16911433728 | bytes 31457280 | tf_op jit(solution)/shard_map/feed_back/pallas_call | solution.py:613
  172.8 4.3 %collective-permute-done.18 = bf16[4,96,3840]{2,1,0:T(8,128)(2,1)S(1)} collective-permute-done((bf16[4,96,3840]{2,1,0:T(8,128)(2,1)}, bf16[4,96,3840]{2,1,0:T(8,128)(2,1)S(1)}, u32[]{:S(2)}, u32[]{:S(2)}) %collective-permute-start.18) | collective-permute-done | bytes 2949152 | tf_op jit(solution)/shard_map/ppermute | solution.py:1004
  178.8 3.4 %add_convert_fusion = bf16[4,96,3840]{2,1,0:T(8,128)(2,1)S(1)} fusion(bf16[4,96,3840]{2,1,0:T(8,128)(2,1)} %copy-done.1, bf16[4,96,3840]{2,1,0:T(8,128)(2,1)} %get-tuple-element.95), kind=kLoop, calls=%fused_computation | loop fusion | flops 5898240 | bytes 8847360 | tf_op jit(solution)/shard_map/convert_element_type | solution.py:1052
  187.7 10.4 %attend_back.1 = (bf16[1024,2304]{1,0:T(8,128)(2,1)}, f32[1,2304]{1,0:T(1,128)}) custom-call(bf16[1024,2304]{1,0:T(8,128)(2,1)} %get-tuple-element.97.joined_ref, bf16[8,6,256,128]{3,2,1,0:T(8,128)(2,1)} %get-tuple-element.98.probs_ref, bf16[1024,768]{1,0:T(8,128)(2,1)} %get-tuple-element.100.ctx_grad_ref), custom_call_target="tpu_custom_call" | custom-call | flops 786432 | bytes 786432 | tf_op jit(solution)/shard_map/attend_back/pallas_call | solution.py:717
  199.7 2.8 collective-permute-done.19
  203.4 3.5 %reduce-scatter.2.cloned.1.call-done = bf16[480,768]{1,0:T(8,128)(2,1)} async-done(((bf16[3840,768]{1,0:T(8,128)(2,1)}), bf16[480,768]{1,0:T(8,128)(2,1)}) %reduce-scatter.2.cloned.1.call-update) | async-done | bytes 737296 | tf_op jit(solution)/shard_map/reduce_scatter | solution.py:1286
  206.9 8.5 %weight_grads.1 = (bf16[4,96,2432]{2,1,0:T(8,128)(2,1)}, bf16[4,96,2432]{2,1,0:T(8,128)(2,1)}) custom-call(s32[3]{0:T(128)} %pad_add_fusion.place_ref, bf16[1024,768]{1,0:T(8,128)(2,1)} %tok_ref.5, bf16[1024,2304]{1,0:T(8,128)(2,1)} %get-tuple-element.103.joined_ref, f32[8,16,128]{2,1,0:T(8,128)} %bitcast.160), custom_call_target="tpu_custom_call" | custom-call | flops 786432 | bytes 786432 | tf_op jit(solution)/shard_map/weight_grads/pallas_call | solution.py:776
  215.4 2.4 collective-permute-start.22
  219.5 2.5 add_convert_fusion.1
  222.0 13.3 %collective-permute-done.22 = bf16[4,24,3840]{2,1,0:T(8,128)(2,1)S(1)} collective-permute-done((bf16[4,24,3840]{2,1,0:T(8,128)(2,1)}, bf16[4,24,3840]{2,1,0:T(8,128)(2,1)S(1)}, u32[]{:S(2)}, u32[]{:S(2)}) %collective-permute-start.22) | collective-permute-done | bytes 737312 | tf_op jit(solution)/shard_map/ppermute | solution.py:1004
  238.8 2.5 collective-permute-start.25
  244.4 2.5 collective-permute-done.23
  246.9 2.4 collective-permute-start.28
  249.3 4.3 %collective-permute-done.24 = bf16[24,3840]{1,0:T(8,128)(2,1)S(1)} collective-permute-done((bf16[24,3840]{1,0:T(8,128)(2,1)S(1)}, bf16[24,3840]{1,0:T(8,128)(2,1)S(1)}, u32[]{:S(2)}, u32[]{:S(2)}) %collective-permute-start.24) | collective-permute-done | bytes 184352 | tf_op jit(solution)/shard_map/ppermute | solution.py:1004
  255.1 9.3 %collective-permute-done.27 = bf16[4,24,2432]{2,1,0:T(8,128)(2,1)S(1)} collective-permute-done((bf16[4,24,2432]{2,1,0:T(8,128)(2,1)S(1)}, bf16[4,24,2432]{2,1,0:T(8,128)(2,1)S(1)}, u32[]{:S(2)}, u32[]{:S(2)}) %collective-permute-start.27) | collective-permute-done | bytes 466976 | tf_op jit(solution)/shard_map/ppermute | solution.py:1004
  272.3 3.2 %collective-permute-done.30 = bf16[24,2432]{1,0:T(8,128)(2,1)S(1)} collective-permute-done((bf16[24,2432]{1,0:T(8,128)(2,1)S(1)}, bf16[24,2432]{1,0:T(8,128)(2,1)S(1)}, u32[]{:S(2)}, u32[]{:S(2)}) %collective-permute-start.30) | collective-permute-done | bytes 116768 | tf_op jit(solution)/shard_map/ppermute | solution.py:1004
  275.6 6.4 %collective-permute-done.33 = bf16[120,768]{1,0:T(8,128)(2,1)S(1)} collective-permute-done((bf16[120,768]{1,0:T(8,128)(2,1)S(1)}, bf16[120,768]{1,0:T(8,128)(2,1)S(1)}, u32[]{:S(2)}, u32[]{:S(2)}) %collective-permute-start.33) | collective-permute-done | bytes 184352 | tf_op jit(solution)/shard_map/ppermute | solution.py:1004
  283.6 2.6 collective-permute-start.36
  287.1 8.7 %input_back.1 = bf16[1024,768]{1,0:T(8,128)(2,1)} custom-call(f32[1024,768]{1,0:T(8,128)} %get-tuple-element.120.inner_ref, bf16[1024,2304]{1,0:T(8,128)(2,1)} %get-tuple-element.103.joined_ref, bf16[4,768,768]{2,1,0:T(8,128)(2,1)} %get-tuple-element.71.w_ref.out_w_ref), custom_call_target="tpu_custom_call" | custom-call | flops 786432 | bytes 786432 | tf_op jit(solution)/shard_map/input_back/pallas_call | solution.py:806
  295.8 2.2 collective-permute-done.36
  (201 shorter events, 66.4 us)
Async XLA Ops:
  7.2 55.5 %all-gather.4.cloned.1.call-start = ((), (), s32[]{:S(2)}) async-start(), calls=%async_computation.1 | async-start | bytes 2654208 | tf_op jit(solution)/shard_map/all_gather | solution.py:1143
  10.9 10.4 %collective-permute-start.1 = (bf16[112,768]{1,0:T(8,128)(2,1)S(1)}, bf16[112,768]{1,0:T(8,128)(2,1)S(1)}, u32[]{:S(2)}, u32[]{:S(2)}) collective-permute-start(bf16[112,768]{1,0:T(8,128)(2,1)S(1)} %constant_dynamic-slice_fusion.4), channel_id=1, source_target_pairs={{0,2},{1,3},{2,4},{3,5},{4,6},{5,7},{6,0},{7,1},{8,10},{9,11},{10,... | collective-permute-start | bytes 516104 | tf_op jit(solution)/shard_map/ppermute | solution.py:1004
  14.0 13.9 %collective-permute-start.2 = (bf16[112,768]{1,0:T(8,128)(2,1)S(1)}, bf16[112,768]{1,0:T(8,128)(2,1)S(1)}, u32[]{:S(2)}, u32[]{:S(2)}) collective-permute-start(bf16[112,768]{1,0:T(8,128)(2,1)S(1)} %constant_dynamic-slice_fusion.4), channel_id=1, source_target_pairs={{0,4},{1,5},{2,6},{3,7},{4,0},{5,1},{6,2},{7,3},{8,12},{9,13},{10,... | collective-permute-start | bytes 516104 | tf_op jit(solution)/shard_map/ppermute | solution.py:1004
  16.6 11.3 %collective-permute-start.3 = (bf16[112,768]{1,0:T(8,128)(2,1)S(1)}, bf16[112,768]{1,0:T(8,128)(2,1)S(1)}, u32[]{:S(2)}, u32[]{:S(2)}) collective-permute-start(bf16[112,768]{1,0:T(8,128)(2,1)S(1)} %constant_dynamic-slice_fusion.4), channel_id=1, source_target_pairs={{0,6},{1,7},{2,0},{3,1},{4,2},{5,3},{6,4},{7,5},{8,14},{9,15},{10,... | collective-permute-start | bytes 516104 | tf_op jit(solution)/shard_map/ppermute | solution.py:1004
  27.9 67.6 %all-gather.6.cloned.1.call-start = ((), (), s32[]{:S(2)}) async-start(), calls=%async_computation.2 | async-start | bytes 2654208 | tf_op jit(solution)/shard_map/all_gather | solution.py:1143
  28.1 13.1 %collective-permute-start.4 = (bf16[288,768]{1,0:T(8,128)(2,1)S(1)}, bf16[288,768]{1,0:T(8,128)(2,1)S(1)}, u32[]{:S(2)}, u32[]{:S(2)}) collective-permute-start(bf16[288,768]{1,0:T(8,128)(2,1)S(1)} %pad_maximum_fusion.4), channel_id=1, source_target_pairs={{0,8},{1,9},{2,10},{3,11},{4,12},{5,13},{6,14},{7,15},{8,0},{9,1},... | collective-permute-start | bytes 1327112 | tf_op jit(solution)/shard_map/ppermute | solution.py:1004
  29.6 21.2 %collective-permute-start.5 = (bf16[288,768]{1,0:T(8,128)(2,1)S(1)}, bf16[288,768]{1,0:T(8,128)(2,1)S(1)}, u32[]{:S(2)}, u32[]{:S(2)}) collective-permute-start(bf16[288,768]{1,0:T(8,128)(2,1)S(1)} %pad_maximum_fusion.4), channel_id=1, source_target_pairs={{0,16},{1,17},{2,18},{3,19},{4,20},{5,21},{6,22},{7,23},{8,24},{9,... | collective-permute-start | bytes 1327112 | tf_op jit(solution)/shard_map/ppermute | solution.py:1004
  31.1 19.7 %collective-permute-start.6 = (bf16[288,768]{1,0:T(8,128)(2,1)S(1)}, bf16[288,768]{1,0:T(8,128)(2,1)S(1)}, u32[]{:S(2)}, u32[]{:S(2)}) collective-permute-start(bf16[288,768]{1,0:T(8,128)(2,1)S(1)} %pad_maximum_fusion.4), channel_id=1, source_target_pairs={{0,24},{1,25},{2,26},{3,27},{4,28},{5,29},{6,30},{7,31},{8,16},{9,... | collective-permute-start | bytes 1327112 | tf_op jit(solution)/shard_map/ppermute | solution.py:1004
  51.6 74.5 %all-gather.8.cloned.1.call-start = ((), (), s32[]{:S(2)}) async-start(), calls=%async_computation.3 | async-start | bytes 1327104 | tf_op jit(solution)/shard_map/all_gather | solution.py:1143
  64.0 21.7 %collective-permute-start.14 = (bf16[576,768]{1,0:T(8,128)(2,1)S(1)}, bf16[576,768]{1,0:T(8,128)(2,1)S(1)}, u32[]{:S(2)}, u32[]{:S(2)}) collective-permute-start(bf16[576,768]{1,0:T(8,128)(2,1)S(1)} %pad_maximum_fusion.1), channel_id=1, source_target_pairs={{0,8},{1,9},{2,10},{3,11},{4,12},{5,13},{6,14},{7,15},{8,0},{9,1},... | collective-permute-start | bytes 2654216 | tf_op jit(solution)/shard_map/ppermute | solution.py:1004
  65.4 21.6 %collective-permute-start.15 = (bf16[576,768]{1,0:T(8,128)(2,1)S(1)}, bf16[576,768]{1,0:T(8,128)(2,1)}, u32[]{:S(2)}, u32[]{:S(2)}) collective-permute-start(bf16[576,768]{1,0:T(8,128)(2,1)S(1)} %pad_maximum_fusion.1), channel_id=1, source_target_pairs={{0,16},{1,17},{2,18},{3,19},{4,20},{5,21},{6,22},{7,23},{8,24},{9,... | collective-permute-start | bytes 2654216 | tf_op jit(solution)/shard_map/ppermute | solution.py:1004
  80.5 126.4 %reduce-scatter.2.cloned.1.call-start = ((), (), s32[]{:S(2)}) async-start(), calls=%async_computation.4 | async-start | bytes 6635520 | tf_op jit(solution)/shard_map/reduce_scatter | solution.py:1286
  85.7 9.8 %collective-permute-start.16 = (bf16[576,768]{1,0:T(8,128)(2,1)S(1)}, bf16[576,768]{1,0:T(8,128)(2,1)}, u32[]{:S(2)}, u32[]{:S(2)}) collective-permute-start(bf16[576,768]{1,0:T(8,128)(2,1)S(1)} %collective-permute-done.14.refs_6_), channel_id=1, source_target_pairs={{0,1},{1,0},{2,3},{3,2},{4,5},{5,4},{6,7},{7,6},{8,9},{9,8},{10,11... | collective-permute-start | bytes 2654216 | tf_op jit(solution)/shard_map/ppermute | solution.py:1004
  87.0 8.6 %collective-permute-start.17 = (bf16[576,768]{1,0:T(8,128)(2,1)}, bf16[576,768]{1,0:T(8,128)(2,1)}, u32[]{:S(2)}, u32[]{:S(2)}) collective-permute-start(bf16[576,768]{1,0:T(8,128)(2,1)} %collective-permute-done.15.refs_7_), channel_id=1, source_target_pairs={{0,1},{1,0},{2,3},{3,2},{4,5},{5,4},{6,7},{7,6},{8,9},{9,8},{10,11... | collective-permute-start | bytes 2654216 | tf_op jit(solution)/shard_map/ppermute | solution.py:1004
  87.0 8.6 %collective-permute-start.12 = (bf16[96,3072]{1,0:T(8,128)(2,1)S(1)}, bf16[96,3072]{1,0:T(8,128)(2,1)S(1)}, u32[]{:S(2)}, u32[]{:S(2)}) collective-permute-start(bf16[96,3072]{1,0:T(8,128)(2,1)S(1)} %copy-done.11), channel_id=1, source_target_pairs={{0,1},{1,0},{2,3},{3,2},{4,5},{5,4},{6,7},{7,6},{8,9},{9,8},{10,11... | collective-permute-start | bytes 1769480 | tf_op jit(solution)/shard_map/ppermute | solution.py:1004
  87.5 8.1 %collective-permute-start.13 = (bf16[384,768]{1,0:T(8,128)(2,1)S(1)}, bf16[384,768]{1,0:T(8,128)(2,1)S(1)}, u32[]{:S(2)}, u32[]{:S(2)}) collective-permute-start(bf16[384,768]{1,0:T(8,128)(2,1)S(1)} %copy-done.13), channel_id=1, source_target_pairs={{0,1},{1,0},{2,3},{3,2},{4,5},{5,4},{6,7},{7,6},{8,9},{9,8},{10,11... | collective-permute-start | bytes 1769480 | tf_op jit(solution)/shard_map/ppermute | solution.py:1004
  183.7 18.8 %collective-permute-start.19 = (bf16[4,24,3840]{2,1,0:T(8,128)(2,1)}, bf16[4,24,3840]{2,1,0:T(8,128)(2,1)}, u32[]{:S(2)}, u32[]{:S(2)}) collective-permute-start(bf16[4,24,3840]{2,1,0:T(8,128)(2,1)} %get-tuple-element.167), channel_id=1, source_target_pairs={{0,8},{1,9},{2,10},{3,11},{4,12},{5,13},{6,14},{7,15},{8,0},{9,1},... | collective-permute-start | bytes 2211848 | tf_op jit(solution)/shard_map/ppermute | solution.py:1004
  184.7 18.7 %collective-permute-start.20 = (bf16[4,24,3840]{2,1,0:T(8,128)(2,1)}, bf16[4,24,3840]{2,1,0:T(8,128)(2,1)}, u32[]{:S(2)}, u32[]{:S(2)}) collective-permute-start(bf16[4,24,3840]{2,1,0:T(8,128)(2,1)} %get-tuple-element.166), channel_id=1, source_target_pairs={{0,16},{1,17},{2,18},{3,19},{4,20},{5,21},{6,22},{7,23},{8,24},{9,... | collective-permute-start | bytes 2211848 | tf_op jit(solution)/shard_map/ppermute | solution.py:1004
  215.4 20.0 %collective-permute-start.22 = (bf16[4,24,3840]{2,1,0:T(8,128)(2,1)}, bf16[4,24,3840]{2,1,0:T(8,128)(2,1)S(1)}, u32[]{:S(2)}, u32[]{:S(2)}) collective-permute-start(bf16[4,24,3840]{2,1,0:T(8,128)(2,1)} %get-tuple-element.114), channel_id=1, source_target_pairs={{0,24},{1,25},{2,26},{3,27},{4,28},{5,29},{6,30},{7,31},{8,16},{9,... | collective-permute-start | bytes 2211848 | tf_op jit(solution)/shard_map/ppermute | solution.py:1004
  237.2 9.8 %collective-permute-start.23 = (bf16[24,3840]{1,0:T(8,128)(2,1)S(1)}, bf16[24,3840]{1,0:T(8,128)(2,1)S(1)}, u32[]{:S(2)}, u32[]{:S(2)}) collective-permute-start(bf16[24,3840]{1,0:T(8,128)(2,1)S(1)} %get-tuple-element.182), channel_id=1, source_target_pairs={{0,2},{1,3},{2,4},{3,5},{4,6},{5,7},{6,0},{7,1},{8,10},{9,11},{10,... | collective-permute-start | bytes 552968 | tf_op jit(solution)/shard_map/ppermute | solution.py:1004
  237.5 16.1 %collective-permute-start.24 = (bf16[24,3840]{1,0:T(8,128)(2,1)S(1)}, bf16[24,3840]{1,0:T(8,128)(2,1)S(1)}, u32[]{:S(2)}, u32[]{:S(2)}) collective-permute-start(bf16[24,3840]{1,0:T(8,128)(2,1)S(1)} %get-tuple-element.181), channel_id=1, source_target_pairs={{0,4},{1,5},{2,6},{3,7},{4,0},{5,1},{6,2},{7,3},{8,12},{9,13},{10,... | collective-permute-start | bytes 552968 | tf_op jit(solution)/shard_map/ppermute | solution.py:1004
  238.8 14.8 %collective-permute-start.25 = (bf16[24,3840]{1,0:T(8,128)(2,1)S(1)}, bf16[24,3840]{1,0:T(8,128)(2,1)S(1)}, u32[]{:S(2)}, u32[]{:S(2)}) collective-permute-start(bf16[24,3840]{1,0:T(8,128)(2,1)S(1)} %get-tuple-element.180), channel_id=1, source_target_pairs={{0,6},{1,7},{2,0},{3,1},{4,2},{5,3},{6,4},{7,5},{8,14},{9,15},{10,... | collective-permute-start | bytes 552968 | tf_op jit(solution)/shard_map/ppermute | solution.py:1004
  241.4 13.7 %collective-permute-start.26 = (bf16[4,24,2432]{2,1,0:T(8,128)(2,1)S(1)}, bf16[4,24,2432]{2,1,0:T(8,128)(2,1)S(1)}, u32[]{:S(2)}, u32[]{:S(2)}) collective-permute-start(bf16[4,24,2432]{2,1,0:T(8,128)(2,1)S(1)} %get-tuple-element.179), channel_id=1, source_target_pairs={{0,8},{1,9},{2,10},{3,11},{4,12},{5,13},{6,14},{7,15},{8,0},{9,1},... | collective-permute-start | bytes 1400840 | tf_op jit(solution)/shard_map/ppermute | solution.py:1004
  243.0 21.5 %collective-permute-start.27 = (bf16[4,24,2432]{2,1,0:T(8,128)(2,1)S(1)}, bf16[4,24,2432]{2,1,0:T(8,128)(2,1)S(1)}, u32[]{:S(2)}, u32[]{:S(2)}) collective-permute-start(bf16[4,24,2432]{2,1,0:T(8,128)(2,1)S(1)} %get-tuple-element.178), channel_id=1, source_target_pairs={{0,16},{1,17},{2,18},{3,19},{4,20},{5,21},{6,22},{7,23},{8,24},{9,... | collective-permute-start | bytes 1400840 | tf_op jit(solution)/shard_map/ppermute | solution.py:1004
  246.9 17.5 %collective-permute-start.28 = (bf16[4,24,2432]{2,1,0:T(8,128)(2,1)S(1)}, bf16[4,24,2432]{2,1,0:T(8,128)(2,1)S(1)}, u32[]{:S(2)}, u32[]{:S(2)}) collective-permute-start(bf16[4,24,2432]{2,1,0:T(8,128)(2,1)S(1)} %get-tuple-element.177), channel_id=1, source_target_pairs={{0,24},{1,25},{2,26},{3,27},{4,28},{5,29},{6,30},{7,31},{8,16},{9,... | collective-permute-start | bytes 1400840 | tf_op jit(solution)/shard_map/ppermute | solution.py:1004
  265.5 10.0 %collective-permute-start.30 = (bf16[24,2432]{1,0:T(8,128)(2,1)S(1)}, bf16[24,2432]{1,0:T(8,128)(2,1)S(1)}, u32[]{:S(2)}, u32[]{:S(2)}) collective-permute-start(bf16[24,2432]{1,0:T(8,128)(2,1)S(1)} %get-tuple-element.185), channel_id=1, source_target_pairs={{0,4},{1,5},{2,6},{3,7},{4,0},{5,1},{6,2},{7,3},{8,12},{9,13},{10,... | collective-permute-start | bytes 350216 | tf_op jit(solution)/shard_map/ppermute | solution.py:1004
  266.9 8.6 %collective-permute-start.29 = (bf16[24,2432]{1,0:T(8,128)(2,1)S(1)}, bf16[24,2432]{1,0:T(8,128)(2,1)S(1)}, u32[]{:S(2)}, u32[]{:S(2)}) collective-permute-start(bf16[24,2432]{1,0:T(8,128)(2,1)S(1)} %get-tuple-element.183), channel_id=1, source_target_pairs={{0,2},{1,3},{2,4},{3,5},{4,6},{5,7},{6,0},{7,1},{8,10},{9,11},{10,... | collective-permute-start | bytes 350216 | tf_op jit(solution)/shard_map/ppermute | solution.py:1004
  270.2 11.7 %collective-permute-start.33 = (bf16[120,768]{1,0:T(8,128)(2,1)S(1)}, bf16[120,768]{1,0:T(8,128)(2,1)S(1)}, u32[]{:S(2)}, u32[]{:S(2)}) collective-permute-start(bf16[120,768]{1,0:T(8,128)(2,1)S(1)} %get-tuple-element.188), channel_id=1, source_target_pairs={{0,16},{1,17},{2,18},{3,19},{4,20},{5,21},{6,22},{7,23},{8,24},{9,... | collective-permute-start | bytes 552968 | tf_op jit(solution)/shard_map/ppermute | solution.py:1004
  271.4 10.5 %collective-permute-start.32 = (bf16[120,768]{1,0:T(8,128)(2,1)S(1)}, bf16[120,768]{1,0:T(8,128)(2,1)S(1)}, u32[]{:S(2)}, u32[]{:S(2)}) collective-permute-start(bf16[120,768]{1,0:T(8,128)(2,1)S(1)} %get-tuple-element.186), channel_id=1, source_target_pairs={{0,8},{1,9},{2,10},{3,11},{4,12},{5,13},{6,14},{7,15},{8,0},{9,1},... | collective-permute-start | bytes 552968 | tf_op jit(solution)/shard_map/ppermute | solution.py:1004
  282.3 13.6 %collective-permute-start.37 = (bf16[24,10112]{1,0:T(8,128)(2,1)S(1)}, bf16[24,10112]{1,0:T(8,128)(2,1)S(1)}, u32[]{:S(2)}, u32[]{:S(2)}) collective-permute-start(bf16[24,10112]{1,0:T(8,128)(2,1)S(1)} %get-tuple-element.194), channel_id=1, source_target_pairs={{0,24},{1,25},{2,26},{3,27},{4,28},{5,29},{6,30},{7,31},{8,16},{9,... | collective-permute-start | bytes 1456136 | tf_op jit(solution)/shard_map/ppermute | solution.py:1004
  283.6 14.5 %collective-permute-start.36 = (bf16[24,10112]{1,0:T(8,128)(2,1)S(1)}, bf16[24,10112]{1,0:T(8,128)(2,1)S(1)}, u32[]{:S(2)}, u32[]{:S(2)}) collective-permute-start(bf16[24,10112]{1,0:T(8,128)(2,1)S(1)} %get-tuple-element.194), channel_id=1, source_target_pairs={{0,16},{1,17},{2,18},{3,19},{4,20},{5,21},{6,22},{7,23},{8,24},{9,... | collective-permute-start | bytes 1456136 | tf_op jit(solution)/shard_map/ppermute | solution.py:1004
  286.2 12.2 %collective-permute-start.35 = (bf16[24,10112]{1,0:T(8,128)(2,1)S(1)}, bf16[24,10112]{1,0:T(8,128)(2,1)S(1)}, u32[]{:S(2)}, u32[]{:S(2)}) collective-permute-start(bf16[24,10112]{1,0:T(8,128)(2,1)S(1)} %get-tuple-element.194), channel_id=1, source_target_pairs={{0,8},{1,9},{2,10},{3,11},{4,12},{5,13},{6,14},{7,15},{8,0},{9,1},... | collective-permute-start | bytes 1456136 | tf_op jit(solution)/shard_map/ppermute | solution.py:1004
  (36 other events, 416.2 us)
Sparse Core Ops, SparseCore 0:
  28.0 34.4 all-gather.3
  64.8 30.7 all-gather.5
  97.2 21.7 all-gather.7
  141.7 65.1 reduce-scatter.1

commit v2 on v1

--- a/solution.py
+++ b/solution.py
@@ -1336,7 +1336,7 @@
     input_grad = input_back(inner, joined_grad, joint)
 
     if direct:
-        up_red.over_far(keep)
+        up_red.over_far(joined_seen)
         joint_red = Reduction(place, keep, send, reps, chips)
         joint_red.over_reps()
         up_red.over_chips(joint_red.both)

time: 315 us -> 315 us (level)
  no operation moved by 1% of the time
where the time goes in v2:
time: 315 us
  Pallas kernels  121 us (38%)
  waiting for transfers between devices  98.9 us (31%)
  starting transfers between devices  41.8 us (13%)
  local copies, waits for them, and re-layouts  20.5 us (7%)
  other arithmetic  16.3 us (5%)
  between operations  15.5 us (5%)
    ppermute x38, waiting for transfers between devices, move(): return lax.ppermute(values, ('rep', 'fsdp'), pairs)  90.1 us
    ppermute x38, starting transfers between devices, move(): return lax.ppermute(values, ('rep', 'fsdp'), pairs)  41.7 us
    pallas_call x1, Pallas kernels, feed_back(): pl.pallas_call(feed_back_kernel, grid=(steps + 1,), in_specs=[pl.BlockSpe...  29.6 us
    pallas_call x1, Pallas kernels, feed(): pl.pallas_call(functools.partial(feed_kernel, length, load, len(weights))...  29.5 us
    pallas_call x1, Pallas kernels, leave(): pl.pallas_call(functools.partial(leave_kernel, length, classes), grid=(st...  15.4 us
    pallas_call x1, Pallas kernels, attend(): pl.pallas_call(functools.partial(attend_kernel, length), grid=(steps,), i...  13.6 us
    pallas_call x1, Pallas kernels, attend_back(): pl.pallas_call(functools.partial(attend_back_kernel, length), grid=(steps...  10.4 us
    pallas_call x1, Pallas kernels, input_back(): pl.pallas_call(input_kernel, grid=(steps,), in_specs=[pl.BlockSpec((block...  8.74 us
  transfers between devices with their start and end apart: 42, of which 25 were waited for; matrix products, arithmetic and copies ran while one was open for 6% of the time, Pallas kernels for 31%

profile of v2, /device:TPU:0, one launch (start us, length us, event | category | flops | bytes accessed | tf_op | source)
XLA Modules:
  0.0 314.6 jit_solution(10765296116749855291)
XLA Ops:
  10.9 3.1 collective-permute-start.1
  14.0 2.6 collective-permute-start.2
  18.8 2.6 collective-permute-done.1.refs_2_
  21.3 6.5 %collective-permute-done.2.refs_3_ = bf16[112,768]{1,0:T(8,128)(2,1)S(1)} collective-permute-done((bf16[112,768]{1,0:T(8,128)(2,1)S(1)}, bf16[112,768]{1,0:T(8,128)(2,1)S(1)}, u32[]{:S(2)}, u32[]{:S(2)}) %collective-permute-start.2) | collective-permute-done | bytes 172064 | tf_op jit(solution)/shard_map/ppermute | solution.py:1004
  32.4 8.8 %collective-permute-done.4.refs_5_ = bf16[288,768]{1,0:T(8,128)(2,1)S(1)} collective-permute-done((bf16[288,768]{1,0:T(8,128)(2,1)S(1)}, bf16[288,768]{1,0:T(8,128)(2,1)S(1)}, u32[]{:S(2)}, u32[]{:S(2)}) %collective-permute-start.4) | collective-permute-done | bytes 442400 | tf_op jit(solution)/shard_map/ppermute | solution.py:1004
  41.2 9.6 %collective-permute-done.5.refs_6_ = bf16[288,768]{1,0:T(8,128)(2,1)S(1)} collective-permute-done((bf16[288,768]{1,0:T(8,128)(2,1)S(1)}, bf16[288,768]{1,0:T(8,128)(2,1)S(1)}, u32[]{:S(2)}, u32[]{:S(2)}) %collective-permute-start.5) | collective-permute-done | bytes 442400 | tf_op jit(solution)/shard_map/ppermute | solution.py:1004
  57.0 5.7 %lay.1 = (bf16[4,768,768]{2,1,0:T(8,128)(2,1)}, f32[16,768]{1,0:T(8,128)}) custom-call(s32[3]{0:T(128)} %pad_add_fusion.place_ref, bf16[112,3072]{1,0:T(8,128)(2,1)} %copy-done, bf16[112,3072]{1,0:T(8,128)(2,1)} %copy-done.3, bf16[112,768]{1,0:T(8,128)(2,1)} %copy-done.4, bf16[112,768]{1,0:T(8,128)(2,1)} %copy-done.5, bf16[112,768]{1,0:T(8,128)(2,1)} %copy-done.6, ...), custom_call_target="tpu_custom_call" | custom-call | bytes 9486336 | tf_op jit(solution)/shard_map/lay/pallas_call | solution.py:969
  66.9 13.6 %attend.1 = (bf16[1024,2304]{1,0:T(8,128)(2,1)}, bf16[8,6,256,128]{3,2,1,0:T(8,128)(2,1)}, bf16[1024,768]{1,0:T(8,128)(2,1)}) custom-call(bf16[1024,768]{1,0:T(8,128)(2,1)} %tok_ref.5, bf16[4,768,768]{2,1,0:T(8,128)(2,1)} %get-tuple-element.71.w_ref.out_w_ref, f32[16,768]{1,0:T(8,128)} %get-tuple-element.72.vec_ref), custom_call_target="tpu_custom_call" | custom-call | flops 4831838208 | bytes 15728640 | tf_op jit(solution)/shard_map/attend/pallas_call | solution.py:134
  80.5 5.2 %collective-permute-done.14.refs_6_ = bf16[576,768]{1,0:T(8,128)(2,1)S(1)} collective-permute-done((bf16[576,768]{1,0:T(8,128)(2,1)S(1)}, bf16[576,768]{1,0:T(8,128)(2,1)S(1)}, u32[]{:S(2)}, u32[]{:S(2)}) %collective-permute-start.14) | collective-permute-done | bytes 884768 | tf_op jit(solution)/shard_map/ppermute | solution.py:1004
  90.3 5.2 %all-gather.6.cloned.1.call-done = bf16[1536,768]{1,0:T(8,128)(2,1)} async-done(((bf16[192,768]{1,0:T(8,128)(2,1)}), bf16[1536,768]{1,0:T(8,128)(2,1)}) %all-gather.6.cloned.1.call-update) | async-done | bytes 2359312 | tf_op jit(solution)/shard_map/all_gather | solution.py:1143
  96.6 29.5 %feed.1 = (bf16[768,1024]{1,0:T(8,128)(2,1)}, bf16[3072,1024]{1,0:T(8,128)(2,1)}, bf16[1024,3072]{1,0:T(8,128)(2,1)}, bf16[1024,768]{1,0:T(8,128)(2,1)}, f32[102...) custom-call(s32[3]{0:T(128)} %pad_add_fusion.place_ref, ...), custom_call_target="tpu_custom_call" | custom-call | flops 10871635968 | bytes 31457280 | tf_op jit(solution)/shard_map/feed/pallas_call | solution.py:300
  126.1 15.4 %leave.1 = (f32[1024,768]{1,0:T(8,128)}, bf16[1024,768]{1,0:T(8,128)(2,1)}, bf16[8,480,768]{2,1,0:T(8,128)(2,1)}, f32[4,768]{1,0:T(4,128)}, f32[8,768]{1,0:T(8,128)}, /*index=5*/f32[8,8]{1,0:T(8,128)}, f32[2,8]{1,0:T(2,128)}) custom-call(s32[8]{0:T(128)} %exit_ref.3, bf16[1024,768]{1,0:T(8,128)(2,1)} %get-tuple-element.142.output_ref, ...), custom_call_target="tpu_custom_call" | custom-call | flops 4831838208 | bytes 23592960 | tf_op jit(solution)/shard_map/leave/pallas_call | solution.py:478
  141.5 29.6 %feed_back.1 = (bf16[4,96,3840]{2,1,0:T(8,128)(2,1)}, bf16[4,96,3840]{2,1,0:T(8,128)(2,1)}, f32[1,3072]{1,0:T(1,128)}, f32[1024,768]{1,0:T(8,128)}, bf16[1024,76...) custom-call(s32[3]{0:T(128)} %pad_add_fusion.place_ref, ...), custom_call_target="tpu_custom_call" | custom-call | flops 16911433728 | bytes 31457280 | tf_op jit(solution)/shard_map/feed_back/pallas_call | solution.py:613
  172.8 4.3 %collective-permute-done.18 = bf16[4,96,3840]{2,1,0:T(8,128)(2,1)S(1)} collective-permute-done((bf16[4,96,3840]{2,1,0:T(8,128)(2,1)}, bf16[4,96,3840]{2,1,0:T(8,128)(2,1)S(1)}, u32[]{:S(2)}, u32[]{:S(2)}) %collective-permute-start.18) | collective-permute-done | bytes 2949152 | tf_op jit(solution)/shard_map/ppermute | solution.py:1004
  178.8 3.4 %add_convert_fusion = bf16[4,96,3840]{2,1,0:T(8,128)(2,1)S(1)} fusion(bf16[4,96,3840]{2,1,0:T(8,128)(2,1)} %copy-done.1, bf16[4,96,3840]{2,1,0:T(8,128)(2,1)} %get-tuple-element.95), kind=kLoop, calls=%fused_computation | loop fusion | flops 5898240 | bytes 8847360 | tf_op jit(solution)/shard_map/convert_element_type | solution.py:1052
  187.7 10.4 %attend_back.1 = (bf16[1024,2304]{1,0:T(8,128)(2,1)}, f32[1,2304]{1,0:T(1,128)}) custom-call(bf16[1024,2304]{1,0:T(8,128)(2,1)} %get-tuple-element.97.joined_ref, bf16[8,6,256,128]{3,2,1,0:T(8,128)(2,1)} %get-tuple-element.98.probs_ref, bf16[1024,768]{1,0:T(8,128)(2,1)} %get-tuple-element.100.ctx_grad_ref), custom_call_target="tpu_custom_call" | custom-call | flops 786432 | bytes 786432 | tf_op jit(solution)/shard_map/attend_back/pallas_call | solution.py:717
  199.7 2.8 collective-permute-done.19
  203.4 3.5 %reduce-scatter.2.cloned.1.call-done = bf16[480,768]{1,0:T(8,128)(2,1)} async-done(((bf16[3840,768]{1,0:T(8,128)(2,1)}), bf16[480,768]{1,0:T(8,128)(2,1)}) %reduce-scatter.2.cloned.1.call-update) | async-done | bytes 737296 | tf_op jit(solution)/shard_map/reduce_scatter | solution.py:1286
  206.9 8.5 %weight_grads.1 = (bf16[4,96,2432]{2,1,0:T(8,128)(2,1)}, bf16[4,96,2432]{2,1,0:T(8,128)(2,1)}) custom-call(s32[3]{0:T(128)} %pad_add_fusion.place_ref, bf16[1024,768]{1,0:T(8,128)(2,1)} %tok_ref.5, bf16[1024,2304]{1,0:T(8,128)(2,1)} %get-tuple-element.103.joined_ref, f32[8,16,128]{2,1,0:T(8,128)} %bitcast.160), custom_call_target="tpu_custom_call" | custom-call | flops 786432 | bytes 786432 | tf_op jit(solution)/shard_map/weight_grads/pallas_call | solution.py:776
  215.4 2.4 collective-permute-start.22
  219.5 2.5 add_convert_fusion.1
  222.0 13.3 %collective-permute-done.22 = bf16[4,24,3840]{2,1,0:T(8,128)(2,1)S(1)} collective-permute-done((bf16[4,24,3840]{2,1,0:T(8,128)(2,1)}, bf16[4,24,3840]{2,1,0:T(8,128)(2,1)S(1)}, u32[]{:S(2)}, u32[]{:S(2)}) %collective-permute-start.22) | collective-permute-done | bytes 737312 | tf_op jit(solution)/shard_map/ppermute | solution.py:1004
  238.8 2.5 collective-permute-start.25
  244.4 2.5 collective-permute-done.23
  246.9 2.4 collective-permute-start.28
  249.3 4.3 %collective-permute-done.24 = bf16[24,3840]{1,0:T(8,128)(2,1)S(1)} collective-permute-done((bf16[24,3840]{1,0:T(8,128)(2,1)S(1)}, bf16[24,3840]{1,0:T(8,128)(2,1)S(1)}, u32[]{:S(2)}, u32[]{:S(2)}) %collective-permute-start.24) | collective-permute-done | bytes 184352 | tf_op jit(solution)/shard_map/ppermute | solution.py:1004
  255.1 9.3 %collective-permute-done.27 = bf16[4,24,2432]{2,1,0:T(8,128)(2,1)S(1)} collective-permute-done((bf16[4,24,2432]{2,1,0:T(8,128)(2,1)S(1)}, bf16[4,24,2432]{2,1,0:T(8,128)(2,1)S(1)}, u32[]{:S(2)}, u32[]{:S(2)}) %collective-permute-start.27) | collective-permute-done | bytes 466976 | tf_op jit(solution)/shard_map/ppermute | solution.py:1004
  272.3 3.2 %collective-permute-done.30 = bf16[24,2432]{1,0:T(8,128)(2,1)S(1)} collective-permute-done((bf16[24,2432]{1,0:T(8,128)(2,1)S(1)}, bf16[24,2432]{1,0:T(8,128)(2,1)S(1)}, u32[]{:S(2)}, u32[]{:S(2)}) %collective-permute-start.30) | collective-permute-done | bytes 116768 | tf_op jit(solution)/shard_map/ppermute | solution.py:1004
  275.6 6.4 %collective-permute-done.33 = bf16[120,768]{1,0:T(8,128)(2,1)S(1)} collective-permute-done((bf16[120,768]{1,0:T(8,128)(2,1)S(1)}, bf16[120,768]{1,0:T(8,128)(2,1)S(1)}, u32[]{:S(2)}, u32[]{:S(2)}) %collective-permute-start.33) | collective-permute-done | bytes 184352 | tf_op jit(solution)/shard_map/ppermute | solution.py:1004
  283.6 2.6 collective-permute-start.36
  287.1 8.7 %input_back.1 = bf16[1024,768]{1,0:T(8,128)(2,1)} custom-call(f32[1024,768]{1,0:T(8,128)} %get-tuple-element.120.inner_ref, bf16[1024,2304]{1,0:T(8,128)(2,1)} %get-tuple-element.103.joined_ref, bf16[4,768,768]{2,1,0:T(8,128)(2,1)} %get-tuple-element.71.w_ref.out_w_ref), custom_call_target="tpu_custom_call" | custom-call | flops 786432 | bytes 786432 | tf_op jit(solution)/shard_map/input_back/pallas_call | solution.py:806
  295.8 2.2 collective-permute-done.36
  (201 shorter events, 66.4 us)
Async XLA Ops:
  7.2 55.5 %all-gather.4.cloned.1.call-start = ((), (), s32[]{:S(2)}) async-start(), calls=%async_computation.1 | async-start | bytes 2654208 | tf_op jit(solution)/shard_map/all_gather | solution.py:1143
  10.9 10.4 %collective-permute-start.1 = (bf16[112,768]{1,0:T(8,128)(2,1)S(1)}, bf16[112,768]{1,0:T(8,128)(2,1)S(1)}, u32[]{:S(2)}, u32[]{:S(2)}) collective-permute-start(bf16[112,768]{1,0:T(8,128)(2,1)S(1)} %constant_dynamic-slice_fusion.4), channel_id=1, source_target_pairs={{0,2},{1,3},{2,4},{3,5},{4,6},{5,7},{6,0},{7,1},{8,10},{9,11},{10,... | collective-permute-start | bytes 516104 | tf_op jit(solution)/shard_map/ppermute | solution.py:1004
  14.0 13.9 %collective-permute-start.2 = (bf16[112,768]{1,0:T(8,128)(2,1)S(1)}, bf16[112,768]{1,0:T(8,128)(2,1)S(1)}, u32[]{:S(2)}, u32[]{:S(2)}) collective-permute-start(bf16[112,768]{1,0:T(8,128)(2,1)S(1)} %constant_dynamic-slice_fusion.4), channel_id=1, source_target_pairs={{0,4},{1,5},{2,6},{3,7},{4,0},{5,1},{6,2},{7,3},{8,12},{9,13},{10,... | collective-permute-start | bytes 516104 | tf_op jit(solution)/shard_map/ppermute | solution.py:1004
  16.6 11.3 %collective-permute-start.3 = (bf16[112,768]{1,0:T(8,128)(2,1)S(1)}, bf16[112,768]{1,0:T(8,128)(2,1)S(1)}, u32[]{:S(2)}, u32[]{:S(2)}) collective-permute-start(bf16[112,768]{1,0:T(8,128)(2,1)S(1)} %constant_dynamic-slice_fusion.4), channel_id=1, source_target_pairs={{0,6},{1,7},{2,0},{3,1},{4,2},{5,3},{6,4},{7,5},{8,14},{9,15},{10,... | collective-permute-start | bytes 516104 | tf_op jit(solution)/shard_map/ppermute | solution.py:1004
  27.9 67.6 %all-gather.6.cloned.1.call-start = ((), (), s32[]{:S(2)}) async-start(), calls=%async_computation.2 | async-start | bytes 2654208 | tf_op jit(solution)/shard_map/all_gather | solution.py:1143
  28.1 13.1 %collective-permute-start.4 = (bf16[288,768]{1,0:T(8,128)(2,1)S(1)}, bf16[288,768]{1,0:T(8,128)(2,1)S(1)}, u32[]{:S(2)}, u32[]{:S(2)}) collective-permute-start(bf16[288,768]{1,0:T(8,128)(2,1)S(1)} %pad_maximum_fusion.4), channel_id=1, source_target_pairs={{0,8},{1,9},{2,10},{3,11},{4,12},{5,13},{6,14},{7,15},{8,0},{9,1},... | collective-permute-start | bytes 1327112 | tf_op jit(solution)/shard_map/ppermute | solution.py:1004
  29.6 21.2 %collective-permute-start.5 = (bf16[288,768]{1,0:T(8,128)(2,1)S(1)}, bf16[288,768]{1,0:T(8,128)(2,1)S(1)}, u32[]{:S(2)}, u32[]{:S(2)}) collective-permute-start(bf16[288,768]{1,0:T(8,128)(2,1)S(1)} %pad_maximum_fusion.4), channel_id=1, source_target_pairs={{0,16},{1,17},{2,18},{3,19},{4,20},{5,21},{6,22},{7,23},{8,24},{9,... | collective-permute-start | bytes 1327112 | tf_op jit(solution)/shard_map/ppermute | solution.py:1004
  31.1 19.7 %collective-permute-start.6 = (bf16[288,768]{1,0:T(8,128)(2,1)S(1)}, bf16[288,768]{1,0:T(8,128)(2,1)S(1)}, u32[]{:S(2)}, u32[]{:S(2)}) collective-permute-start(bf16[288,768]{1,0:T(8,128)(2,1)S(1)} %pad_maximum_fusion.4), channel_id=1, source_target_pairs={{0,24},{1,25},{2,26},{3,27},{4,28},{5,29},{6,30},{7,31},{8,16},{9,... | collective-permute-start | bytes 1327112 | tf_op jit(solution)/shard_map/ppermute | solution.py:1004
  51.6 74.5 %all-gather.8.cloned.1.call-start = ((), (), s32[]{:S(2)}) async-start(), calls=%async_computation.3 | async-start | bytes 1327104 | tf_op jit(solution)/shard_map/all_gather | solution.py:1143
  64.0 21.7 %collective-permute-start.14 = (bf16[576,768]{1,0:T(8,128)(2,1)S(1)}, bf16[576,768]{1,0:T(8,128)(2,1)S(1)}, u32[]{:S(2)}, u32[]{:S(2)}) collective-permute-start(bf16[576,768]{1,0:T(8,128)(2,1)S(1)} %pad_maximum_fusion.1), channel_id=1, source_target_pairs={{0,8},{1,9},{2,10},{3,11},{4,12},{5,13},{6,14},{7,15},{8,0},{9,1},... | collective-permute-start | bytes 2654216 | tf_op jit(solution)/shard_map/ppermute | solution.py:1004
  65.4 21.6 %collective-permute-start.15 = (bf16[576,768]{1,0:T(8,128)(2,1)S(1)}, bf16[576,768]{1,0:T(8,128)(2,1)}, u32[]{:S(2)}, u32[]{:S(2)}) collective-permute-start(bf16[576,768]{1,0:T(8,128)(2,1)S(1)} %pad_maximum_fusion.1), channel_id=1, source_target_pairs={{0,16},{1,17},{2,18},{3,19},{4,20},{5,21},{6,22},{7,23},{8,24},{9,... | collective-permute-start | bytes 2654216 | tf_op jit(solution)/shard_map/ppermute | solution.py:1004
  80.5 126.4 %reduce-scatter.2.cloned.1.call-start = ((), (), s32[]{:S(2)}) async-start(), calls=%async_computation.4 | async-start | bytes 6635520 | tf_op jit(solution)/shard_map/reduce_scatter | solution.py:1286
  85.7 9.8 %collective-permute-start.16 = (bf16[576,768]{1,0:T(8,128)(2,1)S(1)}, bf16[576,768]{1,0:T(8,128)(2,1)}, u32[]{:S(2)}, u32[]{:S(2)}) collective-permute-start(bf16[576,768]{1,0:T(8,128)(2,1)S(1)} %collective-permute-done.14.refs_6_), channel_id=1, source_target_pairs={{0,1},{1,0},{2,3},{3,2},{4,5},{5,4},{6,7},{7,6},{8,9},{9,8},{10,11... | collective-permute-start | bytes 2654216 | tf_op jit(solution)/shard_map/ppermute | solution.py:1004
  87.0 8.6 %collective-permute-start.17 = (bf16[576,768]{1,0:T(8,128)(2,1)}, bf16[576,768]{1,0:T(8,128)(2,1)}, u32[]{:S(2)}, u32[]{:S(2)}) collective-permute-start(bf16[576,768]{1,0:T(8,128)(2,1)} %collective-permute-done.15.refs_7_), channel_id=1, source_target_pairs={{0,1},{1,0},{2,3},{3,2},{4,5},{5,4},{6,7},{7,6},{8,9},{9,8},{10,11... | collective-permute-start | bytes 2654216 | tf_op jit(solution)/shard_map/ppermute | solution.py:1004
  87.0 8.6 %collective-permute-start.12 = (bf16[96,3072]{1,0:T(8,128)(2,1)S(1)}, bf16[96,3072]{1,0:T(8,128)(2,1)S(1)}, u32[]{:S(2)}, u32[]{:S(2)}) collective-permute-start(bf16[96,3072]{1,0:T(8,128)(2,1)S(1)} %copy-done.11), channel_id=1, source_target_pairs={{0,1},{1,0},{2,3},{3,2},{4,5},{5,4},{6,7},{7,6},{8,9},{9,8},{10,11... | collective-permute-start | bytes 1769480 | tf_op jit(solution)/shard_map/ppermute | solution.py:1004
  87.5 8.1 %collective-permute-start.13 = (bf16[384,768]{1,0:T(8,128)(2,1)S(1)}, bf16[384,768]{1,0:T(8,128)(2,1)S(1)}, u32[]{:S(2)}, u32[]{:S(2)}) collective-permute-start(bf16[384,768]{1,0:T(8,128)(2,1)S(1)} %copy-done.13), channel_id=1, source_target_pairs={{0,1},{1,0},{2,3},{3,2},{4,5},{5,4},{6,7},{7,6},{8,9},{9,8},{10,11... | collective-permute-start | bytes 1769480 | tf_op jit(solution)/shard_map/ppermute | solution.py:1004
  183.7 18.8 %collective-permute-start.19 = (bf16[4,24,3840]{2,1,0:T(8,128)(2,1)}, bf16[4,24,3840]{2,1,0:T(8,128)(2,1)}, u32[]{:S(2)}, u32[]{:S(2)}) collective-permute-start(bf16[4,24,3840]{2,1,0:T(8,128)(2,1)} %get-tuple-element.167), channel_id=1, source_target_pairs={{0,8},{1,9},{2,10},{3,11},{4,12},{5,13},{6,14},{7,15},{8,0},{9,1},... | collective-permute-start | bytes 2211848 | tf_op jit(solution)/shard_map/ppermute | solution.py:1004
  184.7 18.7 %collective-permute-start.20 = (bf16[4,24,3840]{2,1,0:T(8,128)(2,1)}, bf16[4,24,3840]{2,1,0:T(8,128)(2,1)}, u32[]{:S(2)}, u32[]{:S(2)}) collective-permute-start(bf16[4,24,3840]{2,1,0:T(8,128)(2,1)} %get-tuple-element.166), channel_id=1, source_target_pairs={{0,16},{1,17},{2,18},{3,19},{4,20},{5,21},{6,22},{7,23},{8,24},{9,... | collective-permute-start | bytes 2211848 | tf_op jit(solution)/shard_map/ppermute | solution.py:1004
  215.4 20.0 %collective-permute-start.22 = (bf16[4,24,3840]{2,1,0:T(8,128)(2,1)}, bf16[4,24,3840]{2,1,0:T(8,128)(2,1)S(1)}, u32[]{:S(2)}, u32[]{:S(2)}) collective-permute-start(bf16[4,24,3840]{2,1,0:T(8,128)(2,1)} %get-tuple-element.114), channel_id=1, source_target_pairs={{0,24},{1,25},{2,26},{3,27},{4,28},{5,29},{6,30},{7,31},{8,16},{9,... | collective-permute-start | bytes 2211848 | tf_op jit(solution)/shard_map/ppermute | solution.py:1004
  237.2 9.8 %collective-permute-start.23 = (bf16[24,3840]{1,0:T(8,128)(2,1)S(1)}, bf16[24,3840]{1,0:T(8,128)(2,1)S(1)}, u32[]{:S(2)}, u32[]{:S(2)}) collective-permute-start(bf16[24,3840]{1,0:T(8,128)(2,1)S(1)} %get-tuple-element.182), channel_id=1, source_target_pairs={{0,2},{1,3},{2,4},{3,5},{4,6},{5,7},{6,0},{7,1},{8,10},{9,11},{10,... | collective-permute-start | bytes 552968 | tf_op jit(solution)/shard_map/ppermute | solution.py:1004
  237.5 16.1 %collective-permute-start.24 = (bf16[24,3840]{1,0:T(8,128)(2,1)S(1)}, bf16[24,3840]{1,0:T(8,128)(2,1)S(1)}, u32[]{:S(2)}, u32[]{:S(2)}) collective-permute-start(bf16[24,3840]{1,0:T(8,128)(2,1)S(1)} %get-tuple-element.181), channel_id=1, source_target_pairs={{0,4},{1,5},{2,6},{3,7},{4,0},{5,1},{6,2},{7,3},{8,12},{9,13},{10,... | collective-permute-start | bytes 552968 | tf_op jit(solution)/shard_map/ppermute | solution.py:1004
  238.8 14.8 %collective-permute-start.25 = (bf16[24,3840]{1,0:T(8,128)(2,1)S(1)}, bf16[24,3840]{1,0:T(8,128)(2,1)S(1)}, u32[]{:S(2)}, u32[]{:S(2)}) collective-permute-start(bf16[24,3840]{1,0:T(8,128)(2,1)S(1)} %get-tuple-element.180), channel_id=1, source_target_pairs={{0,6},{1,7},{2,0},{3,1},{4,2},{5,3},{6,4},{7,5},{8,14},{9,15},{10,... | collective-permute-start | bytes 552968 | tf_op jit(solution)/shard_map/ppermute | solution.py:1004
  241.4 13.7 %collective-permute-start.26 = (bf16[4,24,2432]{2,1,0:T(8,128)(2,1)S(1)}, bf16[4,24,2432]{2,1,0:T(8,128)(2,1)S(1)}, u32[]{:S(2)}, u32[]{:S(2)}) collective-permute-start(bf16[4,24,2432]{2,1,0:T(8,128)(2,1)S(1)} %get-tuple-element.179), channel_id=1, source_target_pairs={{0,8},{1,9},{2,10},{3,11},{4,12},{5,13},{6,14},{7,15},{8,0},{9,1},... | collective-permute-start | bytes 1400840 | tf_op jit(solution)/shard_map/ppermute | solution.py:1004
  243.0 21.5 %collective-permute-start.27 = (bf16[4,24,2432]{2,1,0:T(8,128)(2,1)S(1)}, bf16[4,24,2432]{2,1,0:T(8,128)(2,1)S(1)}, u32[]{:S(2)}, u32[]{:S(2)}) collective-permute-start(bf16[4,24,2432]{2,1,0:T(8,128)(2,1)S(1)} %get-tuple-element.178), channel_id=1, source_target_pairs={{0,16},{1,17},{2,18},{3,19},{4,20},{5,21},{6,22},{7,23},{8,24},{9,... | collective-permute-start | bytes 1400840 | tf_op jit(solution)/shard_map/ppermute | solution.py:1004
  246.9 17.5 %collective-permute-start.28 = (bf16[4,24,2432]{2,1,0:T(8,128)(2,1)S(1)}, bf16[4,24,2432]{2,1,0:T(8,128)(2,1)S(1)}, u32[]{:S(2)}, u32[]{:S(2)}) collective-permute-start(bf16[4,24,2432]{2,1,0:T(8,128)(2,1)S(1)} %get-tuple-element.177), channel_id=1, source_target_pairs={{0,24},{1,25},{2,26},{3,27},{4,28},{5,29},{6,30},{7,31},{8,16},{9,... | collective-permute-start | bytes 1400840 | tf_op jit(solution)/shard_map/ppermute | solution.py:1004
  265.5 10.0 %collective-permute-start.30 = (bf16[24,2432]{1,0:T(8,128)(2,1)S(1)}, bf16[24,2432]{1,0:T(8,128)(2,1)S(1)}, u32[]{:S(2)}, u32[]{:S(2)}) collective-permute-start(bf16[24,2432]{1,0:T(8,128)(2,1)S(1)} %get-tuple-element.185), channel_id=1, source_target_pairs={{0,4},{1,5},{2,6},{3,7},{4,0},{5,1},{6,2},{7,3},{8,12},{9,13},{10,... | collective-permute-start | bytes 350216 | tf_op jit(solution)/shard_map/ppermute | solution.py:1004
  266.9 8.6 %collective-permute-start.29 = (bf16[24,2432]{1,0:T(8,128)(2,1)S(1)}, bf16[24,2432]{1,0:T(8,128)(2,1)S(1)}, u32[]{:S(2)}, u32[]{:S(2)}) collective-permute-start(bf16[24,2432]{1,0:T(8,128)(2,1)S(1)} %get-tuple-element.183), channel_id=1, source_target_pairs={{0,2},{1,3},{2,4},{3,5},{4,6},{5,7},{6,0},{7,1},{8,10},{9,11},{10,... | collective-permute-start | bytes 350216 | tf_op jit(solution)/shard_map/ppermute | solution.py:1004
  270.2 11.7 %collective-permute-start.33 = (bf16[120,768]{1,0:T(8,128)(2,1)S(1)}, bf16[120,768]{1,0:T(8,128)(2,1)S(1)}, u32[]{:S(2)}, u32[]{:S(2)}) collective-permute-start(bf16[120,768]{1,0:T(8,128)(2,1)S(1)} %get-tuple-element.188), channel_id=1, source_target_pairs={{0,16},{1,17},{2,18},{3,19},{4,20},{5,21},{6,22},{7,23},{8,24},{9,... | collective-permute-start | bytes 552968 | tf_op jit(solution)/shard_map/ppermute | solution.py:1004
  271.4 10.5 %collective-permute-start.32 = (bf16[120,768]{1,0:T(8,128)(2,1)S(1)}, bf16[120,768]{1,0:T(8,128)(2,1)S(1)}, u32[]{:S(2)}, u32[]{:S(2)}) collective-permute-start(bf16[120,768]{1,0:T(8,128)(2,1)S(1)} %get-tuple-element.186), channel_id=1, source_target_pairs={{0,8},{1,9},{2,10},{3,11},{4,12},{5,13},{6,14},{7,15},{8,0},{9,1},... | collective-permute-start | bytes 552968 | tf_op jit(solution)/shard_map/ppermute | solution.py:1004
  282.3 13.6 %collective-permute-start.37 = (bf16[24,10112]{1,0:T(8,128)(2,1)S(1)}, bf16[24,10112]{1,0:T(8,128)(2,1)S(1)}, u32[]{:S(2)}, u32[]{:S(2)}) collective-permute-start(bf16[24,10112]{1,0:T(8,128)(2,1)S(1)} %get-tuple-element.194), channel_id=1, source_target_pairs={{0,24},{1,25},{2,26},{3,27},{4,28},{5,29},{6,30},{7,31},{8,16},{9,... | collective-permute-start | bytes 1456136 | tf_op jit(solution)/shard_map/ppermute | solution.py:1004
  283.6 14.5 %collective-permute-start.36 = (bf16[24,10112]{1,0:T(8,128)(2,1)S(1)}, bf16[24,10112]{1,0:T(8,128)(2,1)S(1)}, u32[]{:S(2)}, u32[]{:S(2)}) collective-permute-start(bf16[24,10112]{1,0:T(8,128)(2,1)S(1)} %get-tuple-element.194), channel_id=1, source_target_pairs={{0,16},{1,17},{2,18},{3,19},{4,20},{5,21},{6,22},{7,23},{8,24},{9,... | collective-permute-start | bytes 1456136 | tf_op jit(solution)/shard_map/ppermute | solution.py:1004
  286.2 12.2 %collective-permute-start.35 = (bf16[24,10112]{1,0:T(8,128)(2,1)S(1)}, bf16[24,10112]{1,0:T(8,128)(2,1)S(1)}, u32[]{:S(2)}, u32[]{:S(2)}) collective-permute-start(bf16[24,10112]{1,0:T(8,128)(2,1)S(1)} %get-tuple-element.194), channel_id=1, source_target_pairs={{0,8},{1,9},{2,10},{3,11},{4,12},{5,13},{6,14},{7,15},{8,0},{9,1},... | collective-permute-start | bytes 1456136 | tf_op jit(solution)/shard_map/ppermute | solution.py:1004
  (36 other events, 416.2 us)
Sparse Core Ops, SparseCore 0:
  28.0 34.4 all-gather.3
  64.8 30.7 all-gather.5
  97.2 21.7 all-gather.7
  141.7 65.1 reduce-scatter.1
